TPU v7x, 512 devices: a whole 4x4x16 slice. The times are simulated.
512 devices in a mesh: mem: 16 (over x, z_lo), tile: 32 (over y, z_hi, core).
Axes of the slice: x: 4, y: 4, z: 16 (z_hi: 4, z_lo: 4; z = z_hi * 4 + z_lo), core: 2. Of those that a mesh axis runs over, the one named last changes fastest.
Arguments:
- ensemble: bfloat16 [32, 256, 256, 256], P('mem', None, 'tile'), may hold values from -4 to 4
- control: float32 [32, 256, 256], P('mem', 'tile'), may hold values from -6 to 6
- weights: float32 [32], P('mem'), may hold values from 0.1 to 0.6
- member_band: int32 [32], P('mem'), may hold values from 0 to 3
- spread: float32 [4], replicated, may hold values from 0.05 to 0.24
- advect: float32 [2, 256], replicated, may hold values from -0.9 to 0.9
- damping: float32 [256], replicated, may hold values from 0.02 to 0.2
- innovation: float32 [256, 256, 256], P(None, 'tile'), may hold values from -4 to 4
- obs_weight: float32 [256, 256], P('tile'), may hold values from 0.3 to 27
Outputs:
- grad_control: float32 [32, 256, 256], P('mem', 'tile')
- grad_weight: float32 [32], P('mem')
All inputs are finite; a program needn't handle non-finite values.
Results may differ from a plain program's by a relative error of at most 0.0003.
Values sent between devices are 32-bit elements; how exact they have to be, the bound alone decides.
No kernel may reach another device: no remote copies, remote signals or barrier semaphores. Data moves between devices by JAX's collectives and lax.ppermute only.
A program may use at most 64 MiB of HBM per device.

v0:
```python
import math

import jax
import jax.numpy as jnp
from jax import lax
from jax.sharding import PartitionSpec as P

SWEEPS = 8


def extended_2(cells, sides, width):
    for axis, dim in sides:
        count = lax.axis_size(axis)
        head = lax.slice_in_dim(cells, 0, width, axis=dim)
        tail = lax.slice_in_dim(cells, cells.shape[dim] - width, cells.shape[dim], axis=dim)
        cells = jnp.concatenate(
            [
                lax.ppermute(tail, axis, [(i, (i + 1) % count) for i in range(count)]),
                cells,
                lax.ppermute(head, axis, [((i + 1) % count, i) for i in range(count)]),
            ],
            axis=dim,
        )
    return cells


def in_blocks(shard, dim, count):
    shape = shard.shape
    blocks = shard.reshape(*shape[:dim], count, shape[dim] // count, *shape[dim + 1 :])
    return jnp.moveaxis(blocks, dim, 0)


def sum_at_owner(shard, axis, dim):
    count = lax.axis_size(axis)
    blocks = lax.all_to_all(in_blocks(shard, dim, count), axis, 0, 0, tiled=True)
    return jnp.sum(blocks, axis=0)


def from_everyone(shard, axis):
    copies = jnp.broadcast_to(shard, (lax.axis_size(axis), *shard.shape))
    return lax.all_to_all(copies, axis, split_axis=0, concat_axis=0, tiled=True)


def joined_along(blocks, dim):
    shape = list(blocks.shape[1:])
    shape[dim] *= blocks.shape[0]
    return jnp.moveaxis(blocks, 0, dim).reshape(shape)


def collect(shard, axis, dim):
    blocks = from_everyone(shard, axis)
    return joined_along(blocks, dim)


def of_everyone(shard, axis):
    return from_everyone(shard, axis).sum(axis=0)


def y_pairs(field):
    zero_col = jnp.zeros(field.shape[:-1] + (1,), field.dtype)
    north = jnp.concatenate([field[..., 1:], zero_col], axis=-1)
    south = jnp.concatenate([zero_col, field[..., :-1]], axis=-1)
    return (north, south)


def sweep_once(extended, rates):
    center = extended[:, 1:-1]
    east = extended[:, 2:]
    west = extended[:, :-2]
    north, south = y_pairs(center)
    return center + rates * (east + west + north + south - 4.0 * center)


def localize(field, rates):
    extended = extended_2(field, (("tile", 1),), SWEEPS)
    for sweep in range(SWEEPS):
        extended = sweep_once(extended, rates)
    return extended


def dynamics(field, along_x, along_y, smooth):
    extended = extended_2(field, (("tile", 1),), 1)
    center = extended[:, 1:-1]
    east = extended[:, 2:]
    west = extended[:, :-2]
    north, south = y_pairs(center)
    return (
        center
        - along_x * ((east - west) * 0.5)
        - along_y * ((north - south) * 0.5)
        + smooth * (east + west + north + south - 4.0 * center)
    )


def adjoint_gradient(increment, advect, damping, innovation, obs_weight):
    along_x = advect[0][:, None, None]
    along_y = advect[1][:, None, None]
    smooth = damping[:, None, None]
    forward = dynamics(increment, along_x, along_y, smooth)
    weighted = obs_weight[None] * (forward - innovation)
    return dynamics(weighted, -along_x, -along_y, smooth)


def per_device(
    ensemble, control, weights, member_band, spread, advect, damping, innovation, obs_weight
):
    one_hot = (
        member_band[:, None] == jnp.arange(spread.shape[0], dtype=jnp.int32)[None, :]
    ).astype(jnp.float32)
    rates = jnp.dot(one_hot, spread, precision=lax.Precision.HIGHEST)[:, None, None]
    localized = localize(control, rates)
    scaled = weights[:, None, None] * localized
    partial_value = jnp.sum(ensemble.astype(jnp.float32) * scaled[:, None], axis=0)
    shared = sum_at_owner(partial_value, "mem", 0)
    levels_part = shared.shape[0]
    offset = lax.axis_index("mem") * levels_part
    advect_part = lax.dynamic_slice_in_dim(advect, offset, levels_part, 1)
    damping_part = lax.dynamic_slice_in_dim(damping, offset, levels_part, 0)
    innovation_part = lax.dynamic_slice_in_dim(innovation, offset, levels_part, 0)
    gradient_part = adjoint_gradient(shared, advect_part, damping_part, innovation_part, obs_weight)
    gradient = collect(gradient_part, "mem", 0)
    projected = jnp.sum(ensemble.astype(jnp.float32) * gradient[None], axis=1)
    grad_control = control + localize(weights[:, None, None] * projected, rates)
    local_sums = jnp.sum(localized * projected, axis=(1, 2))
    total_cells = lax.axis_size("tile") * control.shape[1] * control.shape[2] * ensemble.shape[1]
    grad_weight = of_everyone(local_sums, "tile") / math.sqrt(total_cells)
    return (grad_control, grad_weight)


def solution(mesh):
    in_specs = (
        P("mem", None, "tile", None),
        P("mem", "tile", None),
        P("mem"),
        P("mem"),
        P(),
        P(),
        P(),
        P(None, "tile", None),
        P("tile", None),
    )
    out_specs = (P("mem", "tile", None), P("mem"))
    return jax.shard_map(
        per_device, mesh=mesh, in_specs=in_specs, out_specs=out_specs, check_vma=False
    )
```

profile of v0, /device:TPU:1, one launch (start us, length us, event | category | flops | bytes accessed | tf_op | source)
XLA Modules:
  0.0 192.2 jit_solution(5316185096671136057)
XLA Ops:
  0.7 10.3 %collective-permute-start = (f32[2,8,256]{2,1,0:T(8,128)}, f32[2,8,256]{2,1,0:T(8,128)S(1)}, u32[]{:S(2)}, u32[]{:S(2)}) collective-permute-start(f32[2,8,256]{2,1,0:T(8,128)} %param.10), channel_id=1, source_target_pairs={{0,1},{1,2},{2,3},{3,4},{4,5},{5,6},{6,7},{7,8},{8,9},{9,10},{10,1... | collective-permute-start | bytes 49160 | tf_op jit(solution)/shard_map/ppermute | solution.py:18
  11.0 1.9 %collective-permute-start.1 = (f32[2,8,256]{2,1,0:T(8,128)}, f32[2,8,256]{2,1,0:T(8,128)S(1)}, u32[]{:S(2)}, u32[]{:S(2)}) collective-permute-start(f32[2,8,256]{2,1,0:T(8,128)} %param.10), channel_id=1, source_target_pairs={{1,0},{2,1},{3,2},{4,3},{5,4},{6,5},{7,6},{8,7},{9,8},{10,9},{11,1... | collective-permute-start | bytes 49160 | tf_op jit(solution)/shard_map/ppermute | solution.py:20
  12.9 0.9 convolution_bitcast_fusion
  13.8 0.7 constant_dynamic-update-slice_fusion.1
  14.5 5.7 %collective-permute-done.1 = f32[2,8,256]{2,1,0:T(8,128)S(1)} collective-permute-done((f32[2,8,256]{2,1,0:T(8,128)}, f32[2,8,256]{2,1,0:T(8,128)S(1)}, u32[]{:S(2)}, u32[]{:S(2)}) %collective-permute-start.1) | collective-permute-done | bytes 16416 | tf_op jit(solution)/shard_map/ppermute | solution.py:20
  21.6 1.8 fusion
  23.4 8.4 %all-to-all-start = ((f32[16,16,8,256]{3,2,1,0:T(8,128)}), f32[16,16,8,256]{3,2,1,0:T(8,128)}, u32[]{:S(2)}, u32[]{:S(2)}) async-start(f32[16,16,8,256]{3,2,1,0:T(8,128)} %bitcast.15), calls=%async_computation | async-start | bytes 4194304 | tf_op jit(solution)/shard_map/all_to_all | solution.py:35
  31.9 48.8 %all-to-all-done = f32[16,16,8,256]{3,2,1,0:T(8,128)} async-done(((f32[16,16,8,256]{3,2,1,0:T(8,128)}), f32[16,16,8,256]{3,2,1,0:T(8,128)}, u32[]{:S(2)}, u32[]{:S(2)}) %all-to-all-start) | async-done | bytes 2097184 | tf_op jit(solution)/shard_map/all_to_all | solution.py:35
  80.8 1.7 reduce_sum.46
  82.5 1.9 collective-permute-start.2
  84.5 7.5 %collective-permute-start.3 = (f32[16,1,256]{2,1,0:T(1,128)S(1)}, f32[16,1,256]{2,1,0:T(1,128)S(1)}, u32[]{:S(2)}, u32[]{:S(2)}) collective-permute-start(f32[16,1,256]{2,1,0:T(1,128)S(1)} %get-tuple-element.8), channel_id=1, source_target_pairs={{0,1},{1,2},{2,3},{3,4},{4,5},{5,6},{6,7},{7,8},{8,9},{9,10},{10,1... | collective-permute-start | bytes 49160 | tf_op jit(solution)/shard_map/ppermute | solution.py:18
  92.0 0.1 fusion.91
  92.1 5.0 %collective-permute-done.3 = f32[16,1,256]{2,1,0:T(1,128)S(1)} collective-permute-done((f32[16,1,256]{2,1,0:T(1,128)S(1)}, f32[16,1,256]{2,1,0:T(1,128)S(1)}, u32[]{:S(2)}, u32[]{:S(2)}) %collective-permute-start.3) | collective-permute-done | bytes 16416 | tf_op jit(solution)/shard_map/ppermute | solution.py:18
  97.2 1.1 subtract_multiply_fusion
  98.3 10.4 %collective-permute-start.4 = (f32[16,1,256]{2,1,0:T(1,128)S(1)}, f32[16,1,256]{2,1,0:T(1,128)S(1)}, u32[]{:S(2)}, u32[]{:S(2)}) collective-permute-start(f32[16,1,256]{2,1,0:T(1,128)S(1)} %get-tuple-element.5), channel_id=1, source_target_pairs={{1,0},{2,1},{3,2},{4,3},{5,4},{6,5},{7,6},{8,7},{9,8},{10,9},{11,1... | collective-permute-start | bytes 49160 | tf_op jit(solution)/shard_map/ppermute | solution.py:20
  108.7 1.9 collective-permute-start.5
  110.6 0.1 fusion.89
  110.7 1.0 collective-permute-done.5
  111.8 0.2 multiply_add_fusion
  111.9 0.2 broadcast_in_dim.4
  112.1 49.7 %all_to_all.16 = f32[16,16,8,256]{3,2,1,0:T(8,128)S(1)} all-to-all(f32[16,16,8,256]{3,2,1,0:T(8,128)S(1)} %broadcast_in_dim.4), channel_id=1, replica_groups=mesh['mem'=16,'tile'=32] {'mem'}, dimensions={0} | all-to-all | bytes 4194304 | tf_op jit(solution)/shard_map/all_to_all | solution.py:41
  161.8 0.6 fusion.1
  162.4 0.1 multiply_reduce_fusion
  162.5 0.6 broadcast_in_dim.5
  163.1 10.6 %all-to-all-start.2 = ((f32[32,1,2]{2,1,0:T(1,128)}), f32[32,1,2]{2,1,0:T(1,128)S(1)}, u32[]{:S(2)}, u32[]{:S(2)}) async-start(f32[32,1,2]{2,1,0:T(1,128)} %broadcast_in_dim.5), calls=%async_computation.2 | async-start | bytes 32768 | tf_op jit(solution)/shard_map/all_to_all | solution.py:41
  173.8 7.4 %collective-permute-start.6 = (f32[2,8,256]{2,1,0:T(8,128)S(1)}, f32[2,8,256]{2,1,0:T(8,128)S(1)}, u32[]{:S(2)}, u32[]{:S(2)}) collective-permute-start(f32[2,8,256]{2,1,0:T(8,128)S(1)} %get-tuple-element.45), channel_id=1, source_target_pairs={{0,1},{1,2},{2,3},{3,4},{4,5},{5,6},{6,7},{7,8},{8,9},{9,10},{10,1... | collective-permute-start | bytes 49160 | tf_op jit(solution)/shard_map/ppermute | solution.py:18
  181.2 1.9 collective-permute-start.7
  183.1 4.7 %all-to-all-done.2 = f32[32,1,2]{2,1,0:T(1,128)S(1)} async-done(((f32[32,1,2]{2,1,0:T(1,128)}), f32[32,1,2]{2,1,0:T(1,128)S(1)}, u32[]{:S(2)}, u32[]{:S(2)}) %all-to-all-start.2) | async-done | bytes 288 | tf_op jit(solution)/shard_map/all_to_all | solution.py:41
  187.9 0.5 broadcast_multiply_fusion.2
  188.4 1.8 collective-permute-done.7
  190.4 0.1 fusion.11
  191.5 0.7 fusion.77
  (55 shorter events, 2.8 us)
Async XLA Ops:
  0.6 31.2 %copy-start = (f32[2,256]{1,0:T(2,128)S(1)}, f32[2,256]{1,0:T(2,128)}, u32[]{:S(2)}) copy-start(f32[2,256]{1,0:T(2,128)} %param.14) | copy-start | bytes 6148
  0.6 20.8 %copy-start.4 = (f32[2]{0:T(128)S(1)}, f32[2]{0:T(128)}, u32[]{:S(2)}) copy-start(f32[2]{0:T(128)} %param.11) | copy-start | bytes 28
  0.7 20.9 %copy-start.1 = (bf16[2,256,8,256]{3,2,1,0:T(8,128)(2,1)S(1)}, bf16[2,256,8,256]{3,2,1,0:T(8,128)(2,1)}, u32[]{:S(2)}) copy-start(bf16[2,256,8,256]{3,2,1,0:T(8,128)(2,1)} %param.9) | copy-start | bytes 6291460
  0.7 13.1 %collective-permute-start = (f32[2,8,256]{2,1,0:T(8,128)}, f32[2,8,256]{2,1,0:T(8,128)S(1)}, u32[]{:S(2)}, u32[]{:S(2)}) collective-permute-start(f32[2,8,256]{2,1,0:T(8,128)} %param.10), channel_id=1, source_target_pairs={{0,1},{1,2},{2,3},{3,4},{4,5},{5,6},{6,7},{7,8},{8,9},{9,10},{10,1... | collective-permute-start | bytes 49160 | tf_op jit(solution)/shard_map/ppermute | solution.py:18
  11.0 9.2 %collective-permute-start.1 = (f32[2,8,256]{2,1,0:T(8,128)}, f32[2,8,256]{2,1,0:T(8,128)S(1)}, u32[]{:S(2)}, u32[]{:S(2)}) collective-permute-start(f32[2,8,256]{2,1,0:T(8,128)} %param.10), channel_id=1, source_target_pairs={{1,0},{2,1},{3,2},{4,3},{5,4},{6,5},{7,6},{8,7},{9,8},{10,9},{11,1... | collective-permute-start | bytes 49160 | tf_op jit(solution)/shard_map/ppermute | solution.py:20
  23.4 8.4 %copy-start.5 = (f32[256]{0:T(256)S(1)}, f32[256]{0:T(256)}, u32[]{:S(2)}) copy-start(f32[256]{0:T(256)} %param.15) | copy-start | bytes 3076
  23.4 57.4 %all-to-all-start = ((f32[16,16,8,256]{3,2,1,0:T(8,128)}), f32[16,16,8,256]{3,2,1,0:T(8,128)}, u32[]{:S(2)}, u32[]{:S(2)}) async-start(f32[16,16,8,256]{3,2,1,0:T(8,128)} %bitcast.15), calls=%async_computation | async-start | bytes 4194304 | tf_op jit(solution)/shard_map/all_to_all | solution.py:35
  31.8 65.4 %copy-start.3 = (f32[8,256]{1,0:T(8,128)S(1)}, f32[8,256]{1,0:T(8,128)}, u32[]{:S(2)}) copy-start(f32[8,256]{1,0:T(8,128)} %param.17) | copy-start | bytes 24580
  82.5 9.6 %collective-permute-start.2 = (f32[16,1,256]{2,1,0:T(1,128)S(1)}, f32[16,1,256]{2,1,0:T(1,128)S(1)}, u32[]{:S(2)}, u32[]{:S(2)}) collective-permute-start(f32[16,1,256]{2,1,0:T(1,128)S(1)} %get-tuple-element.9), channel_id=1, source_target_pairs={{1,0},{2,1},{3,2},{4,3},{5,4},{6,5},{7,6},{8,7},{9,8},{10,9},{11,1... | collective-permute-start | bytes 49160 | tf_op jit(solution)/shard_map/ppermute | solution.py:20
  84.5 12.7 %collective-permute-start.3 = (f32[16,1,256]{2,1,0:T(1,128)S(1)}, f32[16,1,256]{2,1,0:T(1,128)S(1)}, u32[]{:S(2)}, u32[]{:S(2)}) collective-permute-start(f32[16,1,256]{2,1,0:T(1,128)S(1)} %get-tuple-element.8), channel_id=1, source_target_pairs={{0,1},{1,2},{2,3},{3,4},{4,5},{5,6},{6,7},{7,8},{8,9},{9,10},{10,1... | collective-permute-start | bytes 49160 | tf_op jit(solution)/shard_map/ppermute | solution.py:18
  98.3 12.4 %collective-permute-start.4 = (f32[16,1,256]{2,1,0:T(1,128)S(1)}, f32[16,1,256]{2,1,0:T(1,128)S(1)}, u32[]{:S(2)}, u32[]{:S(2)}) collective-permute-start(f32[16,1,256]{2,1,0:T(1,128)S(1)} %get-tuple-element.5), channel_id=1, source_target_pairs={{1,0},{2,1},{3,2},{4,3},{5,4},{6,5},{7,6},{8,7},{9,8},{10,9},{11,1... | collective-permute-start | bytes 49160 | tf_op jit(solution)/shard_map/ppermute | solution.py:20
  108.7 3.1 %collective-permute-start.5 = (f32[16,1,256]{2,1,0:T(1,128)S(1)}, f32[16,1,256]{2,1,0:T(1,128)S(1)}, u32[]{:S(2)}, u32[]{:S(2)}) collective-permute-start(f32[16,1,256]{2,1,0:T(1,128)S(1)} %get-tuple-element.4), channel_id=1, source_target_pairs={{0,1},{1,2},{2,3},{3,4},{4,5},{5,6},{6,7},{7,8},{8,9},{9,10},{10,1... | collective-permute-start | bytes 49160 | tf_op jit(solution)/shard_map/ppermute | solution.py:18
  162.4 29.1 %copy-start.2 = (f32[2,8,256]{2,1,0:T(8,128)S(1)}, f32[2,8,256]{2,1,0:T(8,128)}, u32[]{:S(2)}) copy-start(f32[2,8,256]{2,1,0:T(8,128)} %param.10) | copy-start | bytes 49156
  163.1 24.7 %all-to-all-start.2 = ((f32[32,1,2]{2,1,0:T(1,128)}), f32[32,1,2]{2,1,0:T(1,128)S(1)}, u32[]{:S(2)}, u32[]{:S(2)}) async-start(f32[32,1,2]{2,1,0:T(1,128)} %broadcast_in_dim.5), calls=%async_computation.2 | async-start | bytes 32768 | tf_op jit(solution)/shard_map/all_to_all | solution.py:41
  173.8 14.7 %collective-permute-start.6 = (f32[2,8,256]{2,1,0:T(8,128)S(1)}, f32[2,8,256]{2,1,0:T(8,128)S(1)}, u32[]{:S(2)}, u32[]{:S(2)}) collective-permute-start(f32[2,8,256]{2,1,0:T(8,128)S(1)} %get-tuple-element.45), channel_id=1, source_target_pairs={{0,1},{1,2},{2,3},{3,4},{4,5},{5,6},{6,7},{7,8},{8,9},{9,10},{10,1... | collective-permute-start | bytes 49160 | tf_op jit(solution)/shard_map/ppermute | solution.py:18
  181.2 9.0 %collective-permute-start.7 = (f32[2,8,256]{2,1,0:T(8,128)S(1)}, f32[2,8,256]{2,1,0:T(8,128)S(1)}, u32[]{:S(2)}, u32[]{:S(2)}) collective-permute-start(f32[2,8,256]{2,1,0:T(8,128)S(1)} %get-tuple-element.45), channel_id=1, source_target_pairs={{1,0},{2,1},{3,2},{4,3},{5,4},{6,5},{7,6},{8,7},{9,8},{10,9},{11,1... | collective-permute-start | bytes 49160 | tf_op jit(solution)/shard_map/ppermute | solution.py:20
where the time goes:
time: 193 us; the launch traced here: 192 us
  waiting for transfers between devices  67 us (35%)
  starting transfers between devices  62.4 us (32%)
  blocking collectives  49.7 us (26%)
  other arithmetic  8.03 us (4%)
  local copies, waits for them, and re-layouts  3.2 us (2%)
    all_to_all x1, blocking collectives, from_everyone(): return lax.all_to_all(copies, axis, split_axis=0, concat_axis=0, tiled=True)  49.7 us
    all_to_all x1, waiting for transfers between devices, sum_at_owner(): lax.all_to_all(in_blocks(shard, dim, count), axis, 0, 0, tiled=True)  48.8 us
    ppermute x4, starting transfers between devices, extended_2(): lax.ppermute(tail, axis, [(i, (i + 1) % count) for i in range(count)])  27.3 us
    ppermute x4, starting transfers between devices, extended_2(): lax.ppermute(head, axis, [((i + 1) % count, i) for i in range(count)])  16.2 us
    all_to_all x1, starting transfers between devices, from_everyone(): return lax.all_to_all(copies, axis, split_axis=0, concat_axis=0, tiled=True)  10.6 us
    all_to_all x1, starting transfers between devices, sum_at_owner(): lax.all_to_all(in_blocks(shard, dim, count), axis, 0, 0, tiled=True)  8.37 us
    ppermute x4, waiting for transfers between devices, extended_2(): lax.ppermute(head, axis, [((i + 1) % count, i) for i in range(count)])  7.42 us
    ppermute x4, waiting for transfers between devices, extended_2(): lax.ppermute(tail, axis, [(i, (i + 1) % count) for i in range(count)])  6.08 us
  transfers between devices with their start and end apart: 10, of which 6 were waited for; matrix products, arithmetic and copies ran while one was open for 1% of the time, Pallas kernels for 0%

commit v1 on v0

v1 whole, which is shorter than its diff:
```python
import functools
import math

import jax
import jax.numpy as jnp
from jax import lax
from jax.experimental import pallas as pl
from jax.experimental.pallas import tpu as pltpu
from jax.sharding import Mesh
from jax.sharding import PartitionSpec as P

SWEEPS = 8
MEM = ("x", "zl")
TILE = ("y", "zh", "core")
T = 96
F32 = jnp.float32
SMEM = pl.BlockSpec(memory_space=pltpu.SMEM)
VMEM = pl.BlockSpec(memory_space=pltpu.VMEM)


def kernel_call(body, ins, outs, scratch=(), name=None):
    return pl.pallas_call(
        body,
        in_specs=[SMEM if s else VMEM for _, s in ins],
        out_specs=[SMEM if s else VMEM for _, s in outs],
        out_shape=[jax.ShapeDtypeStruct(shape, F32) for shape, _ in outs],
        scratch_shapes=list(scratch),
        compiler_params=pltpu.CompilerParams(vmem_limit_bytes=48 * 2**20),
        name=name,
    )(*[a for a, _ in ins])


def y_pair(field):
    lane = lax.broadcasted_iota(jnp.int32, field.shape, field.ndim - 1)
    last = field.shape[-1] - 1
    north = jnp.where(lane == last, 0.0, pltpu.roll(field, last, field.ndim - 1))
    south = jnp.where(lane == 0, 0.0, pltpu.roll(field, 1, field.ndim - 1))
    return north, south


def sweeps(field, rate):
    rows = field.shape[0]
    for _ in range(SWEEPS):
        north, south = y_pair(field)
        east = pltpu.roll(field, rows - 1, 0)
        west = pltpu.roll(field, 1, 0)
        field = field + rate * (east + west + north + south - 4.0 * field)
    return field[8:16]


def strips(core, own, near, far):
    first = core == 0
    above = jnp.where(first, far, near)
    below = jnp.where(first, near, far)
    return jnp.concatenate([above, own, below], axis=0)


def start_kernel(s_planes, pos, band, spread, weights, control, near, far, ens, loc_o, pay_o):
    core = pos[2]
    s4 = s_planes // 4
    scaled = []
    for m in range(2):
        ext = strips(core, control[m], near[8 * m : 8 * m + 8], far[8 * m : 8 * m + 8])
        loc = sweeps(ext, spread[band[m]])
        loc_o[m] = loc
        scaled.append(weights[m] * loc)
        for x in range(4):
            pay_o[x, s4 + m] = scaled[m]
    step = 8 if s4 % 8 == 0 else 4
    for x in range(4):

        def body(i, _, x=x):
            j = pl.multiple_of(i * step, step)
            a = ens[0, pl.ds(x * s4 + j, step)].astype(F32) * scaled[0][None]
            b = ens[1, pl.ds(x * s4 + j, step)].astype(F32) * scaled[1][None]
            pay_o[x, pl.ds(j, step)] = a + b
            return 0

        lax.fori_loop(0, s4 // step, body, 0)


def mid_kernel(s_planes, t_planes, r1, g, pay_o):
    s4, t4 = s_planes // 4, t_planes // 4
    s16, t16 = s4 // 4, t4 // 4
    for z in range(4):
        for j in range(s16):
            k = z * s16 + j
            pay_o[z, j] = (r1[0, k] + r1[1, k]) + (r1[2, k] + r1[3, k])
    scaled = [r1[x, s4 + m] for x in range(4) for m in range(2)]
    for z in range(4):
        for j in range(t16):
            k = z * t16 + j
            pay_o[z, s16 + j] = sum(
                g[x, m, k] * scaled[2 * x + m] for x in range(4) for m in range(2)
            )


def edge_kernel(pos, r2, inc_o, near_o, far_o):
    first = pos[2] == 0
    inc = (r2[0] + r2[1]) + (r2[2] + r2[3])
    inc_o[...] = inc
    head, tail = inc[:, 0:2], inc[:, 6:8]
    near_o[...] = jnp.where(first, tail, head)
    far_o[...] = jnp.where(first, head, tail)


def dynamics_kernel(
    s_planes, t_planes, pos, advect, damping, inc, near, far, innov, obsw, near0, far0,
    grad_o, fields, misfit, seen, weight,
):
    x, z, core = pos[0], pos[1], pos[2]
    first = core == 0
    s16, t16 = s_planes // 16, t_planes // 16
    fields[:, 8:16] = inc[...]
    fields[:, 6:8] = jnp.where(first, far[...], near[...])
    fields[:, 16:18] = jnp.where(first, near[...], far[...])
    seen[:, 8:16] = innov[...]
    above = jnp.where(first, far0[16:32], near0[16:32])
    below = jnp.where(first, near0[16:32], far0[16:32])
    for p in range(16):
        seen[p, 7:8] = above[p : p + 1]
        seen[p, 16:17] = below[p : p + 1]
    weight[8:16] = obsw[...]
    weight[7:8] = jnp.where(first, far0[32:33], near0[32:33])
    weight[16:17] = jnp.where(first, near0[32:33], far0[32:33])
    for p in range(16):
        if p < s16:
            k = (x * 4 + z) * s16 + p
        else:
            k = s_planes + (x * 4 + z) * t16 + (p - s16)
        a, b, e = advect[0, k], advect[1, k], damping[k]
        center, east, west = fields[p, 7:17], fields[p, 8:18], fields[p, 6:16]
        north, south = y_pair(center)
        forward = (
            center
            - a * ((east - west) * 0.5)
            - b * ((north - south) * 0.5)
            + e * (east + west + north + south - 4.0 * center)
        )
        misfit[p, 7:17] = weight[7:17] * (forward - seen[p, 7:17])
        center, east, west = misfit[p, 8:16], misfit[p, 9:17], misfit[p, 7:15]
        north, south = y_pair(center)
        grad_o[p] = (
            center
            + a * ((east - west) * 0.5)
            + b * ((north - south) * 0.5)
            + e * (east + west + north + south - 4.0 * center)
        )


def back_kernel(s_planes, t_planes, g64, g, pay_o):
    s4, t4 = s_planes // 4, t_planes // 4
    s16, t16 = s4 // 4, t4 // 4
    for z in range(4):
        for j in range(s16):
            plane = g64[z, j]
            for x in range(4):
                pay_o[x, z * s16 + j] = plane
    for x in range(4):
        for m in range(2):
            total = None
            for z in range(4):
                part = jnp.sum(g[x, m, z * t16 : (z + 1) * t16] * g64[z, s16:], axis=0)
                total = part if total is None else total + part
            pay_o[x, s4 + m] = total


def project_kernel(s_planes, weights, r3, ens, loc, send_o, sums_o):
    s4 = s_planes // 4
    step = 8 if s4 % 8 == 0 else 4
    totals = []
    for m in range(2):
        totals.append((r3[0, s4 + m] + r3[1, s4 + m]) + (r3[2, s4 + m] + r3[3, s4 + m]))
    for x in range(4):

        def body(i, carry, x=x):
            j = pl.multiple_of(i * step, step)
            grad = r3[x, pl.ds(j, step)]
            return tuple(
                carry[m] + jnp.sum(ens[m, pl.ds(x * s4 + j, step)].astype(F32) * grad, axis=0)
                for m in range(2)
            )

        totals = lax.fori_loop(0, s4 // step, body, tuple(totals))
    for m in range(2):
        send_o[m] = weights[m] * totals[m]
        cells = jnp.sum(loc[m] * totals[m], axis=0, keepdims=True)
        sums_o[:, m : m + 1] = jnp.broadcast_to((cells[:, :128] + cells[:, 128:])[None], (32, 1, 128))


def end_kernel(scale, pos, band, spread, control, send, near, far, sums, out_o, weight_o):
    core = pos[2]
    for m in range(2):
        out_o[m] = control[m] + sweeps(strips(core, send[m], near[m], far[m]), spread[band[m]])
    total = jnp.sum(sums[...], axis=0)
    for m in range(2):
        weight_o[m] = jnp.sum(total[m : m + 1]) * scale


def swap(near, far):
    n = 32
    far_pairs = [(i, (i + 1) % n if i % 2 else (i - 1) % n) for i in range(n)]
    far = lax.ppermute(far, TILE, far_pairs)
    near = lax.ppermute(near, TILE, [(i, i ^ 1) for i in range(n)])
    return near, far


def per_device(
    ensemble, control, weights, member_band, spread, advect, damping, innovation, obs_weight
):
    t, s = T, ensemble.shape[1] - T
    s4, t4, s16, t16 = s // 4, t // 4, s // 16, t // 16
    ix, iz, core = lax.axis_index("x"), lax.axis_index("zl"), lax.axis_index("core")
    pos = jnp.stack([ix, iz, core]).astype(jnp.int32)
    own = ix * 4 + iz

    moved = ensemble[:, s:].astype(F32).reshape(2, 4, t4, 8, 256)
    moved = lax.optimization_barrier(jnp.moveaxis(moved, 1, 0))
    g = lax.all_to_all(moved, "x", 0, 0, tiled=True)

    def edges(row):
        return [
            lax.dynamic_slice(innovation, (own * s16, row, 0), (s16, 1, 256)).reshape(s16, 256),
            lax.dynamic_slice(innovation, (s + own * t16, row, 0), (t16, 1, 256)).reshape(t16, 256),
            lax.dynamic_slice(obs_weight, (row, 0), (1, 256)),
        ]

    strip = control.reshape(16, 256)
    near_row = jnp.where(core == 0, 7, 0)
    near0, far0 = swap(
        jnp.concatenate([strip, *edges(near_row)]), jnp.concatenate([strip, *edges(7 - near_row)])
    )
    loc, pay1 = kernel_call(
        functools.partial(start_kernel, s),
        [(pos, 1), (member_band, 1), (spread, 1), (weights, 1), (control, 0), (near0, 0), (far0, 0), (ensemble, 0)],
        [((2, 8, 256), 0), ((4, s4 + 2, 8, 256), 0)],
        name="start",
    )
    r1 = lax.all_to_all(pay1, "x", 0, 0, tiled=True)
    (pay2,) = kernel_call(
        functools.partial(mid_kernel, s, t), [(r1, 0), (g, 0)], [((4, 16, 8, 256), 0)], name="mid"
    )
    r2 = lax.all_to_all(pay2, "zl", 0, 0, tiled=True)
    inc, near, far = kernel_call(
        edge_kernel, [(pos, 1), (r2, 0)],
        [((16, 8, 256), 0), ((16, 2, 256), 0), ((16, 2, 256), 0)], name="edge",
    )
    near, far = swap(near, far)
    seen = jnp.concatenate(
        [
            lax.dynamic_slice_in_dim(innovation, own * s16, s16, 0),
            lax.dynamic_slice_in_dim(innovation, s + own * t16, t16, 0),
        ]
    )
    (grad,) = kernel_call(
        functools.partial(dynamics_kernel, s, t),
        [(pos, 1), (advect, 1), (damping, 1), (inc, 0), (near, 0), (far, 0), (seen, 0), (obs_weight, 0), (near0, 0), (far0, 0)],
        [((16, 8, 256), 0)],
        [pltpu.VMEM((16, 24, 256), F32)] * 3 + [pltpu.VMEM((24, 256), F32)],
        name="dynamics",
    )
    g64 = lax.all_gather(grad, "zl", axis=0, tiled=False)
    (pay3,) = kernel_call(
        functools.partial(back_kernel, s, t),
        [(g64, 0), (g, 0)], [((4, s4 + 2, 8, 256), 0)], name="back",
    )
    r3 = lax.all_to_all(pay3, "x", 0, 0, tiled=True)
    send, sums = kernel_call(
        functools.partial(project_kernel, s),
        [(weights, 1), (r3, 0), (ensemble, 0), (loc, 0)],
        [((2, 8, 256), 0), ((32, 2, 128), 0)], name="project",
    )
    near, far = swap(send, send)
    sums = lax.all_to_all(sums, TILE, 0, 0, tiled=True)
    cells = 32 * control.shape[1] * control.shape[2] * ensemble.shape[1]
    return tuple(
        kernel_call(
            functools.partial(end_kernel, 1.0 / math.sqrt(cells)),
            [(pos, 1), (member_band, 1), (spread, 1), (control, 0), (send, 0), (near, 0), (far, 0), (sums, 0)],
            [((2, 8, 256), 0), ((2,), 1)], name="end",
        )
    )


def solution(mesh):
    mesh = Mesh(mesh.devices.reshape(4, 4, 4, 4, 2), MEM + TILE)
    in_specs = (
        P(MEM, None, TILE, None),
        P(MEM, TILE, None),
        P(MEM),
        P(MEM),
        P(),
        P(),
        P(),
        P(None, TILE, None),
        P(TILE, None),
    )
    out_specs = (P(MEM, TILE, None), P(MEM))
    return jax.shard_map(
        per_device, mesh=mesh, in_specs=in_specs, out_specs=out_specs, check_vma=False
    )
```

time: 193 us -> 176 us (0.912)
  waiting for transfers between devices: 67 us -> 37.2 us
  local copies, waits for them, and re-layouts: 3.2 us -> 12.2 us
  Pallas kernels: 0 us -> 7.73 us
  other arithmetic: 8.03 us -> 2.17 us
  blocking collectives: 49.7 us -> 52.5 us
    all_to_all x2 -> x3, waiting for transfers between devices: 53.5 us -> 30 us  [the longest x1 16.7 us: per_device(): r1 = lax.all_to_all(pay1, 'x', 0, 0, tiled=True)]
    all_gather x0 -> x1, blocking collectives: none -> 13.6 us  [per_device(): g64 = lax.all_gather(grad, 'zl', axis=0, tiled=False)]
    all_to_all x1 -> x2, blocking collectives: 49.7 us -> 39 us  [the longest x1 22.6 us: per_device(): g = lax.all_to_all(moved, 'x', 0, 0, tiled=True)]
    pallas_call x0 -> x7, Pallas kernels: none -> 7.73 us  [kernel_call(): pl.pallas_call(body, in_specs=[SMEM if s else VMEM for _, s in ins], out_...]
    unnamed x14 -> x32, local copies, waits for them, and re-layouts: 0.76 us -> 7.8 us
    ppermute x8 -> x6, waiting for transfers between devices: 13.5 us -> 7.23 us  [the longest x3 5.66 us: swap(): far = lax.ppermute(far, TILE, far_pairs)]
    all_to_all x2 -> x3, starting transfers between devices: 19 us -> 25 us  [the longest x1 17.3 us: per_device(): sums = lax.all_to_all(sums, TILE, 0, 0, tiled=True)]
    ppermute x8 -> x6, starting transfers between devices: 43.4 us -> 37.5 us  [the longest x3 21.1 us: swap(): far = lax.ppermute(far, TILE, far_pairs)]
  transfers between devices with their start and end apart: 10 -> 9, of which waited for: 6 -> 6; matrix products, arithmetic and copies ran while one was open for 1% -> 2% of each run, Pallas kernels for 0% -> 0%
where the time goes in v1:
time: 176 us; the launch traced here: 175 us
  starting transfers between devices  62.5 us (36%)
  blocking collectives  52.5 us (30%)
  waiting for transfers between devices  37.2 us (21%)
  local copies, waits for them, and re-layouts  12.2 us (7%)
  Pallas kernels  7.73 us (4%)
  other arithmetic  2.17 us (1%)
    all_to_all x1, blocking collectives, per_device(): g = lax.all_to_all(moved, 'x', 0, 0, tiled=True)  22.6 us
    ppermute x3, starting transfers between devices, swap(): far = lax.ppermute(far, TILE, far_pairs)  21.1 us
    all_to_all x1, starting transfers between devices, per_device(): sums = lax.all_to_all(sums, TILE, 0, 0, tiled=True)  17.3 us
    all_to_all x1, waiting for transfers between devices, per_device(): r1 = lax.all_to_all(pay1, 'x', 0, 0, tiled=True)  16.7 us
    ppermute x3, starting transfers between devices, swap(): near = lax.ppermute(near, TILE, [(i, i ^ 1) for i in range(n)])  16.4 us
    all_to_all x1, blocking collectives, per_device(): r3 = lax.all_to_all(pay3, 'x', 0, 0, tiled=True)  16.4 us
    all_gather x1, blocking collectives, per_device(): g64 = lax.all_gather(grad, 'zl', axis=0, tiled=False)  13.6 us
    all_to_all x1, waiting for transfers between devices, per_device(): r2 = lax.all_to_all(pay2, 'zl', 0, 0, tiled=True)  11.3 us
  transfers between devices with their start and end apart: 9, of which 6 were waited for; matrix products, arithmetic and copies ran while one was open for 2% of the time, Pallas kernels for 0%

profile of v1, /device:TPU:1, one launch (start us, length us, event | category | flops | bytes accessed | tf_op | source)
XLA Modules:
  0.0 175.2 jit_solution(2938815417882974384)
XLA Ops:
  0.6 0.8 constant_dynamic-slice_fusion.2
  1.4 0.9 constant_dynamic-slice_fusion.3
  2.3 1.0 constant_dynamic-slice_fusion.4
  4.1 10.2 %collective-permute-start.1 = (f32[33,256]{1,0:T(8,128)S(1)}, f32[33,256]{1,0:T(8,128)S(1)}, u32[]{:S(2)}, u32[]{:S(2)}) collective-permute-start(f32[33,256]{1,0:T(8,128)S(1)} %get-tuple-element.20), channel_id=1, source_target_pairs={{0,31},{1,2},{2,1},{3,4},{4,3},{5,6},{6,5},{7,8},{8,7},{9,10},{10,... | collective-permute-start | bytes 101384 | tf_op jit(solution)/shard_map/ppermute | solution.py:203
  14.3 7.8 %collective-permute-start = (f32[33,256]{1,0:T(8,128)S(1)}, f32[33,256]{1,0:T(8,128)S(1)}, u32[]{:S(2)}, u32[]{:S(2)}) collective-permute-start(f32[33,256]{1,0:T(8,128)S(1)} %get-tuple-element.21), channel_id=1, source_target_pairs={{0,1},{1,0},{2,3},{3,2},{4,5},{5,4},{6,7},{7,6},{8,9},{9,8},{10,11... | collective-permute-start | bytes 101384 | tf_op jit(solution)/shard_map/ppermute | solution.py:204
  23.0 1.6 copy-done
  27.3 1.5 start.1
  28.7 1.1 copy-done.4
  29.8 4.1 %all-to-all-start = ((f32[4,42,8,256]{3,2,1,0:T(8,128)}), f32[4,42,8,256]{3,2,1,0:T(8,128)S(1)}, u32[]{:S(2)}, u32[]{:S(2)}) async-start(f32[4,42,8,256]{3,2,1,0:T(8,128)} %copy-done.4), calls=%async_computation | async-start | bytes 2752512 | tf_op jit(solution)/shard_map/all_to_all | solution.py:239
  34.0 1.3 copy_bitcast_fusion
  35.3 16.7 %all-to-all-done.r1 = f32[4,42,8,256]{3,2,1,0:T(8,128)S(1)} async-done(((f32[4,42,8,256]{3,2,1,0:T(8,128)}), f32[4,42,8,256]{3,2,1,0:T(8,128)S(1)}, u32[]{:S(2)}, u32[]{:S(2)}) %all-to-all-start) | async-done | bytes 1376288 | tf_op jit(solution)/shard_map/all_to_all | solution.py:239
  52.0 1.1 copy-done.2
  53.1 22.6 %all_to_all.25.g = f32[4,2,24,8,256]{4,3,2,1,0:T(8,128)S(1)} all-to-all(f32[4,2,24,8,256]{4,3,2,1,0:T(8,128)} %copy_bitcast_fusion), channel_id=1, replica_groups=mesh['x'=4,'zl'=4,'y'=4,'zh'=4,'core'=2] {'x'}, dimensions={0} | all-to-all | bytes 3145728 | tf_op jit(solution)/shard_map/all_to_all | solution.py:219
  75.7 1.3 copy-done.3
  77.1 1.0 mid.1
  78.0 3.6 %all-to-all-start.2 = ((f32[4,16,8,256]{3,2,1,0:T(8,128)}), f32[4,16,8,256]{3,2,1,0:T(8,128)S(1)}, u32[]{:S(2)}, u32[]{:S(2)}) async-start(f32[4,16,8,256]{3,2,1,0:T(8,128)} %mid.1), calls=%async_computation.2 | async-start | bytes 1048576 | tf_op jit(solution)/shard_map/all_to_all | solution.py:243
  81.6 0.8 constant_dynamic-slice_fusion
  82.4 0.9 constant_dynamic-slice_fusion.1
  83.3 11.3 %all-to-all-done.2.r2 = f32[4,16,8,256]{3,2,1,0:T(8,128)S(1)} async-done(((f32[4,16,8,256]{3,2,1,0:T(8,128)}), f32[4,16,8,256]{3,2,1,0:T(8,128)S(1)}, u32[]{:S(2)}, u32[]{:S(2)}) %all-to-all-start.2) | async-done | bytes 524320 | tf_op jit(solution)/shard_map/all_to_all | solution.py:243
  95.2 4.3 %collective-permute-start.2 = (f32[16,2,256]{2,1,0:T(2,128)S(1)}, f32[16,2,256]{2,1,0:T(2,128)S(1)}, u32[]{:S(2)}, u32[]{:S(2)}) collective-permute-start(f32[16,2,256]{2,1,0:T(2,128)S(1)} %get-tuple-element.11), channel_id=1, source_target_pairs={{0,1},{1,0},{2,3},{3,2},{4,5},{5,4},{6,7},{7,6},{8,9},{9,8},{10,11... | collective-permute-start | bytes 98312 | tf_op jit(solution)/shard_map/ppermute | solution.py:204
  99.5 3.4 %collective-permute-start.3 = (f32[16,2,256]{2,1,0:T(2,128)S(1)}, f32[16,2,256]{2,1,0:T(2,128)S(1)}, u32[]{:S(2)}, u32[]{:S(2)}) collective-permute-start(f32[16,2,256]{2,1,0:T(2,128)S(1)} %get-tuple-element.12), channel_id=1, source_target_pairs={{0,31},{1,2},{2,1},{3,4},{4,3},{5,6},{6,5},{7,8},{8,7},{9,10},{10,... | collective-permute-start | bytes 98312 | tf_op jit(solution)/shard_map/ppermute | solution.py:203
  103.0 5.7 %collective-permute-done.3.far = f32[16,2,256]{2,1,0:T(2,128)S(1)} collective-permute-done((f32[16,2,256]{2,1,0:T(2,128)S(1)}, f32[16,2,256]{2,1,0:T(2,128)S(1)}, u32[]{:S(2)}, u32[]{:S(2)}) %collective-permute-start.3) | collective-permute-done | bytes 32800 | tf_op jit(solution)/shard_map/ppermute | solution.py:203
  108.7 1.2 dynamics.1
  109.9 13.6 %all-gather = f32[64,8,256]{2,1,0:T(8,128)S(1)} all-gather(f32[16,8,256]{2,1,0:T(8,128)S(1)} %dynamics.1), channel_id=2, replica_groups=mesh['x'=4,'zl'=4,'y'=4,'zh'=4,'core'=2] {'zl'}, dimensions={0}, use_global_device_ids=true | all-gather | bytes 655360 | tf_op jit(solution)/shard_map/all_gather | solution.py:262
  123.7 16.4 %all_to_all.26.r3 = f32[4,42,8,256]{3,2,1,0:T(8,128)S(1)} all-to-all(f32[4,42,8,256]{3,2,1,0:T(8,128)S(1)} %back.1), channel_id=1, replica_groups=mesh['x'=4,'zl'=4,'y'=4,'zh'=4,'core'=2] {'x'}, dimensions={0} | all-to-all | bytes 2752512 | tf_op jit(solution)/shard_map/all_to_all | solution.py:267
  140.1 1.6 project.1
  141.6 17.3 %all-to-all-start.4 = ((f32[32,2,128]{2,1,0:T(2,128)}), f32[32,2,128]{2,1,0:T(2,128)S(1)}, u32[]{:S(2)}, u32[]{:S(2)}) async-start(f32[32,2,128]{2,1,0:T(2,128)} %get-tuple-element.15), calls=%async_computation.4 | async-start | bytes 65536 | tf_op jit(solution)/shard_map/all_to_all | solution.py:274
  158.9 7.4 %collective-permute-start.5 = (f32[2,8,256]{2,1,0:T(8,128)S(1)}, f32[2,8,256]{2,1,0:T(8,128)S(1)}, u32[]{:S(2)}, u32[]{:S(2)}) collective-permute-start(f32[2,8,256]{2,1,0:T(8,128)S(1)} %get-tuple-element.14.send), channel_id=1, source_target_pairs={{0,31},{1,2},{2,1},{3,4},{4,3},{5,6},{6,5},{7,8},{8,7},{9,10},{10,... | collective-permute-start | bytes 49160 | tf_op jit(solution)/shard_map/ppermute | solution.py:203
  166.4 4.3 %collective-permute-start.4 = (f32[2,8,256]{2,1,0:T(8,128)S(1)}, f32[2,8,256]{2,1,0:T(8,128)S(1)}, u32[]{:S(2)}, u32[]{:S(2)}) collective-permute-start(f32[2,8,256]{2,1,0:T(8,128)S(1)} %get-tuple-element.14.send), channel_id=1, source_target_pairs={{0,1},{1,0},{2,3},{3,2},{4,5},{5,4},{6,7},{7,6},{8,9},{9,8},{10,11... | collective-permute-start | bytes 49160 | tf_op jit(solution)/shard_map/ppermute | solution.py:204
  170.6 0.8 collective-permute-done.4.near
  171.4 1.9 %all-to-all-done.4.sums = f32[32,2,128]{2,1,0:T(2,128)S(1)} async-done(((f32[32,2,128]{2,1,0:T(2,128)}), f32[32,2,128]{2,1,0:T(2,128)S(1)}, u32[]{:S(2)}, u32[]{:S(2)}) %all-to-all-start.4) | async-done | bytes 32800 | tf_op jit(solution)/shard_map/all_to_all | solution.py:274
  173.4 1.8 %end.1 = (f32[2,8,256]{2,1,0:T(8,128)}, f32[2]{0:T(128)}) custom-call(s32[3]{0:T(128)S(1)} %pad_add_fusion.pos, s32[2]{0:T(128)S(1)} %copy-done.12, f32[4]{0:T(128)S(1)} %copy-done.14, f32[2,8,256]{2,1,0:T(8,128)S(1)} %copy-done.6, f32[2,8,256]{2,1,0:T(8,128)S(1)} %get-tuple-element.14.send, f32[2,8,256]{2,1,0:T(8,128)S(1)} %collective-permute-done.4.near, ...), custom_call_target="tpu_custom_call" | custom-call | tf_op jit(solution)/shard_map/end/pallas_call | solution.py:22
  (41 shorter events, 5.1 us)
Async XLA Ops:
  4.1 18.1 %collective-permute-start.1 = (f32[33,256]{1,0:T(8,128)S(1)}, f32[33,256]{1,0:T(8,128)S(1)}, u32[]{:S(2)}, u32[]{:S(2)}) collective-permute-start(f32[33,256]{1,0:T(8,128)S(1)} %get-tuple-element.20), channel_id=1, source_target_pairs={{0,31},{1,2},{2,1},{3,4},{4,3},{5,6},{6,5},{7,8},{8,7},{9,10},{10,... | collective-permute-start | bytes 101384 | tf_op jit(solution)/shard_map/ppermute | solution.py:203
  14.3 8.7 %collective-permute-start = (f32[33,256]{1,0:T(8,128)S(1)}, f32[33,256]{1,0:T(8,128)S(1)}, u32[]{:S(2)}, u32[]{:S(2)}) collective-permute-start(f32[33,256]{1,0:T(8,128)S(1)} %get-tuple-element.21), channel_id=1, source_target_pairs={{0,1},{1,0},{2,3},{3,2},{4,5},{5,4},{6,7},{7,6},{8,9},{9,8},{10,11... | collective-permute-start | bytes 101384 | tf_op jit(solution)/shard_map/ppermute | solution.py:204
  23.0 1.6 copy-start
  24.6 0.7 copy-start.5
  25.3 0.7 copy-start.9
  25.9 0.7 copy-start.11
  26.6 0.7 copy-start.13
  28.7 1.1 copy-start.4
  29.8 4.1 %slice-start = ((bf16[2,256,8,256]{3,2,1,0:T(8,128)(2,1)}), bf16[2,96,8,256]{3,2,1,0:T(8,128)(2,1)S(1)}, s32[]{:S(2)}) async-start(bf16[2,256,8,256]{3,2,1,0:T(8,128)(2,1)} %ens.3), calls=%async_computation.5 | async-start | bytes 1572864 | tf_op jit(solution)/shard_map/slice | solution.py:217
  29.8 22.2 %all-to-all-start = ((f32[4,42,8,256]{3,2,1,0:T(8,128)}), f32[4,42,8,256]{3,2,1,0:T(8,128)S(1)}, u32[]{:S(2)}, u32[]{:S(2)}) async-start(f32[4,42,8,256]{3,2,1,0:T(8,128)} %copy-done.4), calls=%async_computation | async-start | bytes 2752512 | tf_op jit(solution)/shard_map/all_to_all | solution.py:239
  52.0 1.1 copy-start.2
  75.7 1.3 copy-start.3
  78.0 30.7 %copy-start.7 = (f32[8,256]{1,0:T(8,128)S(1)}, f32[8,256]{1,0:T(8,128)}, u32[]{:S(2)}) copy-start(f32[8,256]{1,0:T(8,128)} %obsw.1) | copy-start | bytes 24580
  78.0 30.7 %copy-start.8 = (f32[2,256]{1,0:T(2,128)S(1)}, f32[2,256]{1,0:T(2,128)}, u32[]{:S(2)}) copy-start(f32[2,256]{1,0:T(2,128)} %advect.1) | copy-start | bytes 6148
  78.0 30.7 %copy-start.15 = (f32[256]{0:T(256)S(1)}, f32[256]{0:T(256)}, u32[]{:S(2)}) copy-start(f32[256]{0:T(256)} %damping.1) | copy-start | bytes 3076
  78.0 16.6 %all-to-all-start.2 = ((f32[4,16,8,256]{3,2,1,0:T(8,128)}), f32[4,16,8,256]{3,2,1,0:T(8,128)S(1)}, u32[]{:S(2)}, u32[]{:S(2)}) async-start(f32[4,16,8,256]{3,2,1,0:T(8,128)} %mid.1), calls=%async_computation.2 | async-start | bytes 1048576 | tf_op jit(solution)/shard_map/all_to_all | solution.py:243
  95.2 7.8 %collective-permute-start.2 = (f32[16,2,256]{2,1,0:T(2,128)S(1)}, f32[16,2,256]{2,1,0:T(2,128)S(1)}, u32[]{:S(2)}, u32[]{:S(2)}) collective-permute-start(f32[16,2,256]{2,1,0:T(2,128)S(1)} %get-tuple-element.11), channel_id=1, source_target_pairs={{0,1},{1,0},{2,3},{3,2},{4,5},{5,4},{6,7},{7,6},{8,9},{9,8},{10,11... | collective-permute-start | bytes 98312 | tf_op jit(solution)/shard_map/ppermute | solution.py:204
  99.5 9.1 %collective-permute-start.3 = (f32[16,2,256]{2,1,0:T(2,128)S(1)}, f32[16,2,256]{2,1,0:T(2,128)S(1)}, u32[]{:S(2)}, u32[]{:S(2)}) collective-permute-start(f32[16,2,256]{2,1,0:T(2,128)S(1)} %get-tuple-element.12), channel_id=1, source_target_pairs={{0,31},{1,2},{2,1},{3,4},{4,3},{5,6},{6,5},{7,8},{8,7},{9,10},{10,... | collective-permute-start | bytes 98312 | tf_op jit(solution)/shard_map/ppermute | solution.py:203
  123.6 16.4 %copy-start.1 = (bf16[2,256,8,256]{3,2,1,0:T(8,128)(2,1)S(1)}, bf16[2,256,8,256]{3,2,1,0:T(8,128)(2,1)}, u32[]{:S(2)}) copy-start(bf16[2,256,8,256]{3,2,1,0:T(8,128)(2,1)} %ens.3) | copy-start | bytes 6291460
  123.7 16.4 %copy-start.10 = (f32[2]{0:T(128)S(1)}, f32[2]{0:T(128)}, u32[]{:S(2)}) copy-start(f32[2]{0:T(128)} %weights.3) | copy-start | bytes 28
  140.0 33.4 %copy-start.6 = (f32[2,8,256]{2,1,0:T(8,128)S(1)}, f32[2,8,256]{2,1,0:T(8,128)}, u32[]{:S(2)}) copy-start(f32[2,8,256]{2,1,0:T(8,128)} %control.3) | copy-start | bytes 49156
  140.0 33.4 %copy-start.12 = (s32[2]{0:T(128)S(1)}, s32[2]{0:T(128)}, u32[]{:S(2)}) copy-start(s32[2]{0:T(128)} %band.3) | copy-start | bytes 28
  140.0 33.4 %copy-start.14 = (f32[4]{0:T(128)S(1)}, f32[4]{0:T(128)}, u32[]{:S(2)}) copy-start(f32[4]{0:T(128)} %spread.3) | copy-start | bytes 52
  141.6 31.8 %all-to-all-start.4 = ((f32[32,2,128]{2,1,0:T(2,128)}), f32[32,2,128]{2,1,0:T(2,128)S(1)}, u32[]{:S(2)}, u32[]{:S(2)}) async-start(f32[32,2,128]{2,1,0:T(2,128)} %get-tuple-element.15), calls=%async_computation.4 | async-start | bytes 65536 | tf_op jit(solution)/shard_map/all_to_all | solution.py:274
  158.9 11.7 %collective-permute-start.5 = (f32[2,8,256]{2,1,0:T(8,128)S(1)}, f32[2,8,256]{2,1,0:T(8,128)S(1)}, u32[]{:S(2)}, u32[]{:S(2)}) collective-permute-start(f32[2,8,256]{2,1,0:T(8,128)S(1)} %get-tuple-element.14.send), channel_id=1, source_target_pairs={{0,31},{1,2},{2,1},{3,4},{4,3},{5,6},{6,5},{7,8},{8,7},{9,10},{10,... | collective-permute-start | bytes 49160 | tf_op jit(solution)/shard_map/ppermute | solution.py:203
  166.4 5.1 %collective-permute-start.4 = (f32[2,8,256]{2,1,0:T(8,128)S(1)}, f32[2,8,256]{2,1,0:T(8,128)S(1)}, u32[]{:S(2)}, u32[]{:S(2)}) collective-permute-start(f32[2,8,256]{2,1,0:T(8,128)S(1)} %get-tuple-element.14.send), channel_id=1, source_target_pairs={{0,1},{1,0},{2,3},{3,2},{4,5},{5,4},{6,7},{7,6},{8,9},{9,8},{10,11... | collective-permute-start | bytes 49160 | tf_op jit(solution)/shard_map/ppermute | solution.py:204

commit v2 on v0

v2 whole, which is shorter than its diff:
```python
import functools
import math

import jax
import jax.numpy as jnp
from jax import lax
from jax.experimental import pallas as pl
from jax.experimental.pallas import tpu as pltpu
from jax.sharding import Mesh
from jax.sharding import PartitionSpec as P

SWEEPS = 8
AXES = ("x", "zp", "zq", "y", "zh", "core")
MEM = ("x", "zp", "zq")
GROUP = ("x", "zq")
TILE = ("y", "zh", "core")
F32 = jnp.float32


def smem():
    return pl.BlockSpec(memory_space=pltpu.SMEM)


def whole(shape):
    return pl.BlockSpec(shape, lambda *i: (0,) * len(shape))


def call(body, name, grid, ins, outs, scratch=(), vmem=40 * 2**20):
    return pl.pallas_call(
        body,
        grid=grid,
        in_specs=[s for _, s in ins],
        out_specs=[s for _, s in outs],
        out_shape=[jax.ShapeDtypeStruct(shape, F32) for shape, _ in outs],
        scratch_shapes=list(scratch),
        compiler_params=pltpu.CompilerParams(vmem_limit_bytes=vmem),
        name=name,
    )(*[a for a, _ in ins])


def y_pair(field):
    lane = lax.broadcasted_iota(jnp.int32, field.shape, field.ndim - 1)
    last = field.shape[-1] - 1
    north = jnp.where(lane == last, 0.0, pltpu.roll(field, last, field.ndim - 1))
    south = jnp.where(lane == 0, 0.0, pltpu.roll(field, 1, field.ndim - 1))
    return north, south


def sweeps(field, rate):
    rows = field.shape[0]
    for _ in range(SWEEPS):
        north, south = y_pair(field)
        east = pltpu.roll(field, rows - 1, 0)
        west = pltpu.roll(field, 1, 0)
        field = field + rate * (east + west + north + south - 4.0 * field)
    return field[8:16]


def strips(first, own, near, far):
    above = jnp.where(first, far, near)
    below = jnp.where(first, near, far)
    return jnp.concatenate([above, own, below], axis=0)


def bring_kernel(ens, control, ens_o, control_o, sem):
    copies = [
        pltpu.make_async_copy(ens, ens_o, sem.at[0]),
        pltpu.make_async_copy(control, control_o, sem.at[1]),
    ]
    for copy in copies:
        copy.start()
    for copy in copies:
        copy.wait()


def start_kernel(pos, scal, control, far, near, ens, loc_o, part_o):
    scaled = []
    for m in range(2):
        loc = sweeps(strips(pos[0] == 0, control[m], near[m], far[m]), scal[m])
        loc_o[m] = loc
        scaled.append(scal[2 + m] * loc)
    n = part_o.shape[1]
    for b in range(8):
        slot = lax.bitwise_xor(jnp.int32(b), pos[2])
        for j in range(0, n, 8):
            k = b * n + j
            part_o[slot, j : j + 8] = (
                ens[0, k : k + 8].astype(F32) * scaled[0][None]
                + ens[1, k : k + 8].astype(F32) * scaled[1][None]
            )


def tree(parts):
    while len(parts) > 1:
        parts = [p + q for p, q in zip(parts[::2], parts[1::2])]
    return parts[0]


def mid_kernel(parts, sum_o):
    n = sum_o.shape[0]
    for j in range(0, n, 4):
        sum_o[j : j + 4] = tree([parts[b, j : j + 4] for b in range(8)])


def edge_kernel(pos, keep, got, seen, obsw, inc_o, far_o, near_o):
    first = pos[0] == 0
    n = inc_o.shape[0]
    for p in range(n):
        inc = keep[p] + got[p]
        inc_o[p] = inc
        see = seen[p]
        head = (inc[0:1], inc[1:2], see[0:1])
        tail = (inc[6:7], inc[7:8], see[7:8])
        for j in range(3):
            near_o[n * j + p : n * j + p + 1] = jnp.where(first, tail[j], head[j])
            far_o[n * j + p : n * j + p + 1] = jnp.where(first, head[j], tail[j])
    head, tail = obsw[0:1], obsw[7:8]
    near_o[3 * n : 3 * n + 1] = jnp.where(first, tail, head)
    far_o[3 * n : 3 * n + 1] = jnp.where(first, head, tail)


def dynamics_kernel(pos, advect, damping, inc, far, near, seen, obsw, out, fields, misfit, see, weight):
    n = inc.shape[0]

    first = pos[0] == 0
    fields[:, 8:16] = inc[...]
    see[:, 8:16] = seen[...]
    above = jnp.where(first, far[...], near[...])
    below = jnp.where(first, near[...], far[...])
    weight[8:16] = obsw[...]
    weight[7:8] = above[3 * n : 3 * n + 1]
    weight[16:17] = below[3 * n : 3 * n + 1]
    own = pos[1]
    for p in range(n):
        k = own * n + p
        fields[p, 6:7] = above[p : p + 1]
        fields[p, 7:8] = above[n + p : n + 1 + p]
        see[p, 7:8] = above[2 * n + p : 2 * n + 1 + p]
        fields[p, 16:17] = below[p : p + 1]
        fields[p, 17:18] = below[n + p : n + 1 + p]
        see[p, 16:17] = below[2 * n + p : 2 * n + 1 + p]
        ax, ay, e = advect[0, k], advect[1, k], damping[k]
        center, east, west = fields[p, 7:17], fields[p, 8:18], fields[p, 6:16]
        north, south = y_pair(center)
        forward = (
            center
            - ax * ((east - west) * 0.5)
            - ay * ((north - south) * 0.5)
            + e * (east + west + north + south - 4.0 * center)
        )
        misfit[p, 7:17] = weight[7:17] * (forward - see[p, 7:17])
        center, east, west = misfit[p, 8:16], misfit[p, 9:17], misfit[p, 7:15]
        north, south = y_pair(center)
        grad = (
            center
            + ax * ((east - west) * 0.5)
            + ay * ((north - south) * 0.5)
            + e * (east + west + north + south - 4.0 * center)
        )
        for b in range(8):
            out[b, p] = grad


def project_kernel(pos, scal, grad, ens, loc, send_o, sums_o, total):
    step = pl.program_id(0)
    n = grad.shape[1]

    @pl.when(step == 0)
    def _():
        total[...] = jnp.zeros_like(total)

    first = lax.bitwise_xor(step, pos[2]) * n
    for m in range(2):
        parts = [
            jnp.sum(ens[m, pl.ds(first + j, 8)].astype(F32) * grad[0, j : j + 8], axis=0)
            for j in range(0, n, 8)
        ]
        total[m] += tree(parts)

    @pl.when(step == pl.num_programs(0) - 1)
    def _():
        for m in range(2):
            send_o[m] = scal[2 + m] * total[m]
            cells = jnp.sum(loc[m] * total[m], axis=0, keepdims=True)
            cells = cells[:, :128] + cells[:, 128:]
            sums_o[:, m : m + 1] = jnp.broadcast_to(cells[None], (32, 1, 128))


def end_kernel(scale, pos, scal, control, send, far, near, sums, out_o, weight_o):
    for m in range(2):
        out_o[m] = control[m] + sweeps(strips(pos[0] == 0, send[m], near[m], far[m]), scal[m])
    total = jnp.sum(sums[...], axis=0)
    for m in range(2):
        weight_o[m] = jnp.sum(total[m : m + 1]) * scale


def swap_tiles(near, far):
    n = 32
    far_pairs = [(i, (i + 1) % n if i % 2 else (i - 1) % n) for i in range(n)]
    far = lax.ppermute(far, TILE, far_pairs)
    near = lax.ppermute(near, TILE, [(i, i ^ 1) for i in range(n)])
    return near, far


def per_device(
    ensemble, control, weights, member_band, spread, advect, damping, innovation, obs_weight
):
    n = ensemble.shape[1] // 8
    ix, zp, zq, core = (lax.axis_index(a) for a in ("x", "zp", "zq", "core"))
    own = ix * 2 + lax.bitwise_xor(zp, zq)
    pos = jnp.stack([core, own, zp]).astype(jnp.int32)
    one_hot = member_band[:, None] == jnp.arange(spread.shape[0], dtype=jnp.int32)[None, :]
    rates = jnp.sum(jnp.where(one_hot, spread[None], 0.0), axis=1)
    scal = jnp.concatenate([rates, weights])
    strip2, planes, rows = (2, 8, 256), (n, 8, 256), (3 * n + 1, 256)
    w2, wn, w4, row_spec = whole(strip2), whole(planes), whole((4, 8, 256)), whole(rows)
    strip_spec = whole((8, 256))

    hbm = pl.BlockSpec(memory_space=pltpu.HBM)
    vmem = pl.BlockSpec(memory_space=pltpu.VMEM)
    ens, own_control = pl.pallas_call(
        bring_kernel,
        in_specs=[hbm, hbm],
        out_specs=[vmem, vmem],
        out_shape=[jax.ShapeDtypeStruct(a.shape, a.dtype) for a in (ensemble, control)],
        scratch_shapes=[pltpu.SemaphoreType.DMA((2,))],
        compiler_params=pltpu.CompilerParams(vmem_limit_bytes=40 * 2**20),
        name="bring",
    )(ensemble, control)
    near0, far0 = swap_tiles(control, control)
    loc, parts = call(
        start_kernel, "start", (1,),
        [(pos, smem()), (scal, smem()), (own_control, w2), (far0, w2), (near0, w2), (ens, whole(ens.shape))],
        [(strip2, w2), ((8, n, 8, 256), whole((8, n, 8, 256)))],
    )
    parts = lax.all_to_all(parts, GROUP, 0, 0, tiled=True)
    (part,) = call(mid_kernel, "mid", (1,), [(parts, whole(parts.shape))], [(planes, wn)])
    got = lax.ppermute(part, ("zp", "zq"), [(0, 3), (3, 0), (1, 2), (2, 1)])
    seen = lax.dynamic_slice_in_dim(innovation, own * n, n, 0)
    inc, far, near = call(
        edge_kernel, "edge", (1,),
        [(pos, smem()), (part, wn), (got, wn), (seen, wn), (obs_weight, strip_spec)],
        [(planes, wn), (rows, row_spec), (rows, row_spec)],
    )
    near, far = swap_tiles(near, far)
    (grad,) = call(
        dynamics_kernel, "dynamics", (1,),
        [(pos, smem()), (advect, smem()), (damping, smem()), (inc, wn), (far, row_spec),
         (near, row_spec), (seen, wn), (obs_weight, strip_spec)],
        [((8, n, 8, 256), whole((8, n, 8, 256)))],
        [pltpu.VMEM((n, 24, 256), F32)] * 3 + [pltpu.VMEM((24, 256), F32)],
    )
    grad = lax.all_to_all(grad, GROUP, 0, 0, tiled=True)
    send, sums = call(
        project_kernel, "project", (8,),
        [(pos, smem()), (scal, smem()),
         (grad, pl.BlockSpec((1, n, 8, 256), lambda b: (b, 0, 0, 0))),
         (ensemble, whole(ensemble.shape)), (loc, w2)],
        [(strip2, w2), ((32, 2, 128), whole((32, 2, 128)))],
        [pltpu.VMEM(strip2, F32)],
    )
    near, far = swap_tiles(send, send)
    sums = lax.all_to_all(sums, TILE, 0, 0, tiled=True)
    cells = 32 * control.shape[1] * control.shape[2] * ensemble.shape[1]
    return tuple(
        call(
            functools.partial(end_kernel, 1.0 / math.sqrt(cells)), "end", (1,),
            [(pos, smem()), (scal, smem()), (control, w2), (send, w2), (far, w2), (near, w2),
             (sums, whole(sums.shape))],
            [(strip2, w2), ((2,), smem())],
        )
    )


def solution(mesh):
    mesh = Mesh(mesh.devices.reshape(4, 2, 2, 4, 4, 2), AXES)
    in_specs = (
        P(MEM, None, TILE, None),
        P(MEM, TILE, None),
        P(MEM),
        P(MEM),
        P(),
        P(),
        P(),
        P(None, TILE, None),
        P(TILE, None),
    )
    out_specs = (P(MEM, TILE, None), P(MEM))
    return jax.shard_map(
        per_device, mesh=mesh, in_specs=in_specs, out_specs=out_specs, check_vma=False
    )
```

time: 193 us -> 141 us (0.73)
  waiting for transfers between devices: 67 us -> 13.7 us
  blocking collectives: 49.7 us -> 60.8 us
  starting transfers between devices: 62.4 us -> 52.1 us
  Pallas kernels: 0 us -> 8.91 us
  other arithmetic: 8.03 us -> 1.66 us
    all_to_all x2 -> x1, waiting for transfers between devices: 53.5 us -> 1.94 us  [per_device(): sums = lax.all_to_all(sums, TILE, 0, 0, tiled=True)]
    all_to_all x1 -> x2, blocking collectives: 49.7 us -> 60.8 us  [the longest x1 31 us: per_device(): parts = lax.all_to_all(parts, GROUP, 0, 0, tiled=True)]
    pallas_call x0 -> x7, Pallas kernels: none -> 8.91 us  [the longest x6 8.74 us: call(): pl.pallas_call(body, grid=grid, in_specs=[s for _, s in ins], out_specs=[...]
    all_to_all x2 -> x1, starting transfers between devices: 19 us -> 11.6 us  [per_device(): sums = lax.all_to_all(sums, TILE, 0, 0, tiled=True)]
    reduce_sum x5 -> x1, other arithmetic: 4.29 us -> 0.85 us  [per_device(): rates = jnp.sum(jnp.where(one_hot, spread[None], 0.0), axis=1)]
    ppermute x8 -> x7, starting transfers between devices: 43.4 us -> 40.5 us  [the longest x3 22.1 us: swap_tiles(): far = lax.ppermute(far, TILE, far_pairs)]
    add x16 -> x0, other arithmetic: 2.07 us -> none  [the longest x14 1.21 us: sweep_once(): return center + rates * (east + west + north + south - 4.0 * center)]
    ppermute x8 -> x7, waiting for transfers between devices: 13.5 us -> 11.8 us  [the longest x1 7.29 us: per_device(): got = lax.ppermute(part, ('zp', 'zq'), [(0, 3), (3, 0), (1, 2), (2, 1)])]
  transfers between devices with their start and end apart: 10 -> 8, of which waited for: 6 -> 4; matrix products, arithmetic and copies ran while one was open for 1% -> 1% of each run, Pallas kernels for 0% -> 0%
where the time goes in v2:
time: 141 us; the launch traced here: 140 us
  blocking collectives  60.8 us (43%)
  starting transfers between devices  52.1 us (37%)
  waiting for transfers between devices  13.7 us (10%)
  Pallas kernels  8.91 us (6%)
  local copies, waits for them, and re-layouts  2.36 us (2%)
  other arithmetic  1.66 us (1%)
    all_to_all x1, blocking collectives, per_device(): parts = lax.all_to_all(parts, GROUP, 0, 0, tiled=True)  31 us
    all_to_all x1, blocking collectives, per_device(): grad = lax.all_to_all(grad, GROUP, 0, 0, tiled=True)  29.7 us
    ppermute x3, starting transfers between devices, swap_tiles(): far = lax.ppermute(far, TILE, far_pairs)  22.1 us
    ppermute x3, starting transfers between devices, swap_tiles(): near = lax.ppermute(near, TILE, [(i, i ^ 1) for i in range(n)])  15.2 us
    all_to_all x1, starting transfers between devices, per_device(): sums = lax.all_to_all(sums, TILE, 0, 0, tiled=True)  11.6 us
    pallas_call x6, Pallas kernels, call(): pl.pallas_call(body, grid=grid, in_specs=[s for _, s in ins], out_specs=[...  8.74 us
    ppermute x1, waiting for transfers between devices, per_device(): got = lax.ppermute(part, ('zp', 'zq'), [(0, 3), (3, 0), (1, 2), (2, 1)])  7.29 us
    ppermute x3, waiting for transfers between devices, swap_tiles(): far = lax.ppermute(far, TILE, far_pairs)  3.68 us
  transfers between devices with their start and end apart: 8, of which 4 were waited for; matrix products, arithmetic and copies ran while one was open for 1% of the time, Pallas kernels for 0%

profile of v2, /device:TPU:1, one launch (start us, length us, event | category | flops | bytes accessed | tf_op | source)
XLA Modules:
  0.0 140.3 jit_solution(13912209593386287762)
XLA Ops:
  0.6 0.0 copy-start
  0.6 10.3 %collective-permute-start = (f32[2,8,256]{2,1,0:T(8,128)}, f32[2,8,256]{2,1,0:T(8,128)S(1)}, u32[]{:S(2)}, u32[]{:S(2)}) collective-permute-start(f32[2,8,256]{2,1,0:T(8,128)} %control.3), channel_id=1, source_target_pairs={{0,31},{1,2},{2,1},{3,4},{4,3},{5,6},{6,5},{7,8},{8,7},{9,10},{10,... | collective-permute-start | bytes 49160 | tf_op jit(solution)/shard_map/ppermute | solution.py:200
  11.0 7.8 %collective-permute-start.1 = (f32[2,8,256]{2,1,0:T(8,128)}, f32[2,8,256]{2,1,0:T(8,128)S(1)}, u32[]{:S(2)}, u32[]{:S(2)}) collective-permute-start(f32[2,8,256]{2,1,0:T(8,128)} %control.3), channel_id=1, source_target_pairs={{0,1},{1,0},{2,3},{3,2},{4,5},{5,4},{6,7},{7,6},{8,9},{9,8},{10,11... | collective-permute-start | bytes 49160 | tf_op jit(solution)/shard_map/ppermute | solution.py:201
  18.8 0.9 fusion
  19.7 0.7 pad_maximum_fusion.scal
  20.4 0.1 pad_add_fusion.pos
  20.5 1.6 %copy-done.1 = bf16[2,256,8,256]{3,2,1,0:T(8,128)(2,1)S(1)} copy-done((bf16[2,256,8,256]{3,2,1,0:T(8,128)(2,1)S(1)}, bf16[2,256,8,256]{3,2,1,0:T(8,128)(2,1)}, u32[]{:S(2)}) %copy-start.1) | copy-done | bytes 2097176
  22.1 0.7 copy-done.3
  22.8 0.2 bring.1
  23.0 0.0 collective-permute-done.far
  23.0 0.0 collective-permute-done.1.near
  23.0 1.6 %start.1 = (f32[2,8,256]{2,1,0:T(8,128)S(1)}, f32[8,32,8,256]{3,2,1,0:T(8,128)S(1)}) custom-call(s32[3]{0:T(128)S(1)} %pad_add_fusion.pos, f32[4]{0:T(128)S(1)} %pad_maximum_fusion.scal, f32[2,8,256]{2,1,0:T(8,128)S(1)} %get-tuple-element.11.control, f32[2,8,256]{2,1,0:T(8,128)S(1)} %collective-permute-done.far, ...), custom_call_target="tpu_custom_call" | custom-call | tf_op jit(solution)/shard_map/start/pallas_call | solution.py:29
  24.7 31.0 %all_to_all.15.parts = f32[8,32,8,256]{3,2,1,0:T(8,128)S(1)} all-to-all(f32[8,32,8,256]{3,2,1,0:T(8,128)S(1)} %get-tuple-element.13), channel_id=1, replica_groups=mesh['x'=4,'zp'=2,'zq'=2,'y'=4,'zh'=4,'core'=2] {'x','zq'}, dimensions={0} | all-to-all | bytes 4194304 | tf_op jit(solution)/shard_map/all_to_all | solution.py:236
  55.7 0.1 mid.1.keep
  55.8 3.1 %collective-permute-start.2 = (f32[32,8,256]{2,1,0:T(8,128)S(1)}, f32[32,8,256]{2,1,0:T(8,128)S(1)}, u32[]{:S(2)}, u32[]{:S(2)}) collective-permute-start(f32[32,8,256]{2,1,0:T(8,128)S(1)} %mid.1.keep), channel_id=1, source_target_pairs={{0,96},{96,0},{32,64},{64,32},{1,97},{97,1},{33,65},{65,33},{2,98}... | collective-permute-start | bytes 786440 | tf_op jit(solution)/shard_map/ppermute | solution.py:238
  59.0 7.3 %collective-permute-done.2.got = f32[32,8,256]{2,1,0:T(8,128)S(1)} collective-permute-done((f32[32,8,256]{2,1,0:T(8,128)S(1)}, f32[32,8,256]{2,1,0:T(8,128)S(1)}, u32[]{:S(2)}, u32[]{:S(2)}) %collective-permute-start.2) | collective-permute-done | bytes 262176 | tf_op jit(solution)/shard_map/ppermute | solution.py:238
  66.3 0.7 edge.1
  67.0 4.3 %collective-permute-start.3 = (f32[97,256]{1,0:T(8,128)S(1)}, f32[97,256]{1,0:T(8,128)S(1)}, u32[]{:S(2)}, u32[]{:S(2)}) collective-permute-start(f32[97,256]{1,0:T(8,128)S(1)} %get-tuple-element.15), channel_id=1, source_target_pairs={{0,31},{1,2},{2,1},{3,4},{4,3},{5,6},{6,5},{7,8},{8,7},{9,10},{10,... | collective-permute-start | bytes 297992 | tf_op jit(solution)/shard_map/ppermute | solution.py:200
  71.3 3.1 %collective-permute-start.4 = (f32[97,256]{1,0:T(8,128)S(1)}, f32[97,256]{1,0:T(8,128)S(1)}, u32[]{:S(2)}, u32[]{:S(2)}) collective-permute-start(f32[97,256]{1,0:T(8,128)S(1)} %get-tuple-element.16), channel_id=1, source_target_pairs={{0,1},{1,0},{2,3},{3,2},{4,5},{5,4},{6,7},{7,6},{8,9},{9,8},{10,11... | collective-permute-start | bytes 297992 | tf_op jit(solution)/shard_map/ppermute | solution.py:201
  74.5 3.7 %collective-permute-done.3.far = f32[97,256]{1,0:T(8,128)S(1)} collective-permute-done((f32[97,256]{1,0:T(8,128)S(1)}, f32[97,256]{1,0:T(8,128)S(1)}, u32[]{:S(2)}, u32[]{:S(2)}) %collective-permute-start.3) | collective-permute-done | bytes 99360 | tf_op jit(solution)/shard_map/ppermute | solution.py:200
  78.2 0.0 collective-permute-done.4.near
  78.2 2.6 %dynamics.1 = f32[8,32,8,256]{3,2,1,0:T(8,128)S(1)} custom-call(s32[3]{0:T(128)S(1)} %pad_add_fusion.pos, f32[2,256]{1,0:T(2,128)S(1)} %copy-done.6, f32[256]{0:T(256)S(1)} %copy-done.7, f32[32,8,256]{2,1,0:T(8,128)S(1)} %get-tuple-element.14.inc, f32[97,256]{1,0:T(8,128)S(1)} %collective-permute-done.3.far, f32[97,256]{1,0:T(8,128)S(1)} %collective-permute-done.4.near, ...), custom_call_target="tpu_custom_call" | custom-call | tf_op jit(solution)/shard_map/dynamics/pallas_call | solution.py:29
  80.8 0.0 copy-start.2
  80.8 29.7 %all_to_all.16.grad = f32[8,32,8,256]{3,2,1,0:T(8,128)S(1)} all-to-all(f32[8,32,8,256]{3,2,1,0:T(8,128)S(1)} %dynamics.1), channel_id=1, replica_groups=mesh['x'=4,'zp'=2,'zq'=2,'y'=4,'zh'=4,'core'=2] {'x','zq'}, dimensions={0} | all-to-all | bytes 4194304 | tf_op jit(solution)/shard_map/all_to_all | solution.py:253
  110.6 1.9 %project.1 = (f32[2,8,256]{2,1,0:T(8,128)S(1)}, f32[32,2,128]{2,1,0:T(2,128)}) custom-call(s32[3]{0:T(128)S(1)} %pad_add_fusion.pos, f32[4]{0:T(128)S(1)} %pad_maximum_fusion.scal, f32[8,32,8,256]{3,2,1,0:T(8,128)S(1)} %all_to_all.16.grad, bf16[2,256,8,256]{3,2,1,0:T(8,128)(2,1)S(1)} %copy-done.2, f32[2,8,256]{2,1,0:T(8,128)S(1)} %get-tuple-element.17.loc), custom_call_target="tpu_custom_call" | custom-call | tf_op jit(solution)/shard_map/project/pallas_call | solution.py:29
  112.4 11.6 %all-to-all-start.2 = ((f32[32,2,128]{2,1,0:T(2,128)}), f32[32,2,128]{2,1,0:T(2,128)S(1)}, u32[]{:S(2)}, u32[]{:S(2)}) async-start(f32[32,2,128]{2,1,0:T(2,128)} %get-tuple-element.19), calls=%async_computation.2 | async-start | bytes 65536 | tf_op jit(solution)/shard_map/all_to_all | solution.py:263
  124.1 7.4 %collective-permute-start.5 = (f32[2,8,256]{2,1,0:T(8,128)S(1)}, f32[2,8,256]{2,1,0:T(8,128)S(1)}, u32[]{:S(2)}, u32[]{:S(2)}) collective-permute-start(f32[2,8,256]{2,1,0:T(8,128)S(1)} %get-tuple-element.18.send), channel_id=1, source_target_pairs={{0,31},{1,2},{2,1},{3,4},{4,3},{5,6},{6,5},{7,8},{8,7},{9,10},{10,... | collective-permute-start | bytes 49160 | tf_op jit(solution)/shard_map/ppermute | solution.py:200
  131.5 4.3 %collective-permute-start.6 = (f32[2,8,256]{2,1,0:T(8,128)S(1)}, f32[2,8,256]{2,1,0:T(8,128)S(1)}, u32[]{:S(2)}, u32[]{:S(2)}) collective-permute-start(f32[2,8,256]{2,1,0:T(8,128)S(1)} %get-tuple-element.18.send), channel_id=1, source_target_pairs={{0,1},{1,0},{2,3},{3,2},{4,5},{5,4},{6,7},{7,6},{8,9},{9,8},{10,11... | collective-permute-start | bytes 49160 | tf_op jit(solution)/shard_map/ppermute | solution.py:201
  135.8 0.0 collective-permute-done.5.far
  135.8 0.8 collective-permute-done.6.near
  136.6 1.9 %all-to-all-done.2.sums = f32[32,2,128]{2,1,0:T(2,128)S(1)} async-done(((f32[32,2,128]{2,1,0:T(2,128)}), f32[32,2,128]{2,1,0:T(2,128)S(1)}, u32[]{:S(2)}, u32[]{:S(2)}) %all-to-all-start.2) | async-done | bytes 32800 | tf_op jit(solution)/shard_map/all_to_all | solution.py:263
  138.6 1.8 %end.1 = (f32[2,8,256]{2,1,0:T(8,128)}, f32[2]{0:T(128)}) custom-call(s32[3]{0:T(128)S(1)} %pad_add_fusion.pos, f32[4]{0:T(128)S(1)} %pad_maximum_fusion.scal, f32[2,8,256]{2,1,0:T(8,128)S(1)} %copy-done.4, f32[2,8,256]{2,1,0:T(8,128)S(1)} %get-tuple-element.18.send, f32[2,8,256]{2,1,0:T(8,128)S(1)} %collective-permute-done.5.far, ...), custom_call_target="tpu_custom_call" | custom-call | tf_op jit(solution)/shard_map/end/pallas_call | solution.py:29
  (13 shorter events, 0.0 us)
Async XLA Ops:
  0.6 58.3 %copy-start = (f32[256,8,256]{2,1,0:T(8,128)S(1)}, f32[256,8,256]{2,1,0:T(8,128)}, u32[]{:S(2)}) copy-start(f32[256,8,256]{2,1,0:T(8,128)} %param.16) | copy-start | bytes 6291460
  0.6 22.4 %collective-permute-start = (f32[2,8,256]{2,1,0:T(8,128)}, f32[2,8,256]{2,1,0:T(8,128)S(1)}, u32[]{:S(2)}, u32[]{:S(2)}) collective-permute-start(f32[2,8,256]{2,1,0:T(8,128)} %control.3), channel_id=1, source_target_pairs={{0,31},{1,2},{2,1},{3,4},{4,3},{5,6},{6,5},{7,8},{8,7},{9,10},{10,... | collective-permute-start | bytes 49160 | tf_op jit(solution)/shard_map/ppermute | solution.py:200
  11.0 12.0 %collective-permute-start.1 = (f32[2,8,256]{2,1,0:T(8,128)}, f32[2,8,256]{2,1,0:T(8,128)S(1)}, u32[]{:S(2)}, u32[]{:S(2)}) collective-permute-start(f32[2,8,256]{2,1,0:T(8,128)} %control.3), channel_id=1, source_target_pairs={{0,1},{1,0},{2,3},{3,2},{4,5},{5,4},{6,7},{7,6},{8,9},{9,8},{10,11... | collective-permute-start | bytes 49160 | tf_op jit(solution)/shard_map/ppermute | solution.py:201
  20.5 1.6 %copy-start.1 = (bf16[2,256,8,256]{3,2,1,0:T(8,128)(2,1)S(1)}, bf16[2,256,8,256]{3,2,1,0:T(8,128)(2,1)}, u32[]{:S(2)}) copy-start(bf16[2,256,8,256]{3,2,1,0:T(8,128)(2,1)} %ens.3) | copy-start | bytes 6291460
  22.1 0.7 copy-start.3
  55.7 10.6 %copy-start.5 = (f32[8,256]{1,0:T(8,128)S(1)}, f32[8,256]{1,0:T(8,128)}, u32[]{:S(2)}) copy-start(f32[8,256]{1,0:T(8,128)} %obsw.3) | copy-start | bytes 24580
  55.7 22.5 %copy-start.6 = (f32[2,256]{1,0:T(2,128)S(1)}, f32[2,256]{1,0:T(2,128)}, u32[]{:S(2)}) copy-start(f32[2,256]{1,0:T(2,128)} %advect.1) | copy-start | bytes 6148
  55.7 22.5 %copy-start.7 = (f32[256]{0:T(256)S(1)}, f32[256]{0:T(256)}, u32[]{:S(2)}) copy-start(f32[256]{0:T(256)} %damping.1) | copy-start | bytes 3076
  55.8 10.5 %collective-permute-start.2 = (f32[32,8,256]{2,1,0:T(8,128)S(1)}, f32[32,8,256]{2,1,0:T(8,128)S(1)}, u32[]{:S(2)}, u32[]{:S(2)}) collective-permute-start(f32[32,8,256]{2,1,0:T(8,128)S(1)} %mid.1.keep), channel_id=1, source_target_pairs={{0,96},{96,0},{32,64},{64,32},{1,97},{97,1},{33,65},{65,33},{2,98}... | collective-permute-start | bytes 786440 | tf_op jit(solution)/shard_map/ppermute | solution.py:238
  67.0 11.2 %collective-permute-start.3 = (f32[97,256]{1,0:T(8,128)S(1)}, f32[97,256]{1,0:T(8,128)S(1)}, u32[]{:S(2)}, u32[]{:S(2)}) collective-permute-start(f32[97,256]{1,0:T(8,128)S(1)} %get-tuple-element.15), channel_id=1, source_target_pairs={{0,31},{1,2},{2,1},{3,4},{4,3},{5,6},{6,5},{7,8},{8,7},{9,10},{10,... | collective-permute-start | bytes 297992 | tf_op jit(solution)/shard_map/ppermute | solution.py:200
  71.3 6.8 %collective-permute-start.4 = (f32[97,256]{1,0:T(8,128)S(1)}, f32[97,256]{1,0:T(8,128)S(1)}, u32[]{:S(2)}, u32[]{:S(2)}) collective-permute-start(f32[97,256]{1,0:T(8,128)S(1)} %get-tuple-element.16), channel_id=1, source_target_pairs={{0,1},{1,0},{2,3},{3,2},{4,5},{5,4},{6,7},{7,6},{8,9},{9,8},{10,11... | collective-permute-start | bytes 297992 | tf_op jit(solution)/shard_map/ppermute | solution.py:201
  80.8 29.7 %copy-start.2 = (bf16[2,256,8,256]{3,2,1,0:T(8,128)(2,1)S(1)}, bf16[2,256,8,256]{3,2,1,0:T(8,128)(2,1)}, u32[]{:S(2)}) copy-start(bf16[2,256,8,256]{3,2,1,0:T(8,128)(2,1)} %ens.3) | copy-start | bytes 6291460
  110.5 28.0 %copy-start.4 = (f32[2,8,256]{2,1,0:T(8,128)S(1)}, f32[2,8,256]{2,1,0:T(8,128)}, u32[]{:S(2)}) copy-start(f32[2,8,256]{2,1,0:T(8,128)} %control.3) | copy-start | bytes 49156
  112.4 26.1 %all-to-all-start.2 = ((f32[32,2,128]{2,1,0:T(2,128)}), f32[32,2,128]{2,1,0:T(2,128)S(1)}, u32[]{:S(2)}, u32[]{:S(2)}) async-start(f32[32,2,128]{2,1,0:T(2,128)} %get-tuple-element.19), calls=%async_computation.2 | async-start | bytes 65536 | tf_op jit(solution)/shard_map/all_to_all | solution.py:263
  124.1 11.7 %collective-permute-start.5 = (f32[2,8,256]{2,1,0:T(8,128)S(1)}, f32[2,8,256]{2,1,0:T(8,128)S(1)}, u32[]{:S(2)}, u32[]{:S(2)}) collective-permute-start(f32[2,8,256]{2,1,0:T(8,128)S(1)} %get-tuple-element.18.send), channel_id=1, source_target_pairs={{0,31},{1,2},{2,1},{3,4},{4,3},{5,6},{6,5},{7,8},{8,7},{9,10},{10,... | collective-permute-start | bytes 49160 | tf_op jit(solution)/shard_map/ppermute | solution.py:200
  131.5 5.1 %collective-permute-start.6 = (f32[2,8,256]{2,1,0:T(8,128)S(1)}, f32[2,8,256]{2,1,0:T(8,128)S(1)}, u32[]{:S(2)}, u32[]{:S(2)}) collective-permute-start(f32[2,8,256]{2,1,0:T(8,128)S(1)} %get-tuple-element.18.send), channel_id=1, source_target_pairs={{0,1},{1,0},{2,3},{3,2},{4,5},{5,4},{6,7},{7,6},{8,9},{9,8},{10,11... | collective-permute-start | bytes 49160 | tf_op jit(solution)/shard_map/ppermute | solution.py:201

commit v3 on v2

v3 whole, which is shorter than its diff:
```python
import functools
import math

import jax
import jax.numpy as jnp
from jax import lax
from jax.experimental import pallas as pl
from jax.experimental.pallas import tpu as pltpu
from jax.sharding import Mesh
from jax.sharding import PartitionSpec as P

SWEEPS = 8
AXES = ("x", "zp", "zq", "y", "zh", "core")
MEM = ("x", "zp", "zq")
GROUP = ("x", "zq")
TILE = ("y", "zh", "core")
F32 = jnp.float32


def smem():
    return pl.BlockSpec(memory_space=pltpu.SMEM)


def whole(shape):
    return pl.BlockSpec(shape, lambda *i: (0,) * len(shape))


def call(body, name, grid, ins, outs, scratch=(), vmem=40 * 2**20):
    return pl.pallas_call(
        body,
        grid=grid,
        in_specs=[s for _, s in ins],
        out_specs=[s for _, s in outs],
        out_shape=[jax.ShapeDtypeStruct(shape, F32) for shape, _ in outs],
        scratch_shapes=list(scratch),
        compiler_params=pltpu.CompilerParams(vmem_limit_bytes=vmem),
        name=name,
    )(*[a for a, _ in ins])


def y_pair(field):
    lane = lax.broadcasted_iota(jnp.int32, field.shape, field.ndim - 1)
    last = field.shape[-1] - 1
    north = jnp.where(lane == last, 0.0, pltpu.roll(field, last, field.ndim - 1))
    south = jnp.where(lane == 0, 0.0, pltpu.roll(field, 1, field.ndim - 1))
    return north, south


def rate_of(pos, scal, m):
    rate = scal[2]
    for b in range(1, scal.shape[0] - 2):
        rate = jnp.where(pos[3 + m] == b, scal[2 + b], rate)
    return rate


def sweeps(field, rate):
    rows = field.shape[0]
    for _ in range(SWEEPS):
        north, south = y_pair(field)
        east = pltpu.roll(field, rows - 1, 0)
        west = pltpu.roll(field, 1, 0)
        field = field + rate * (east + west + north + south - 4.0 * field)
    return field[8:16]


def strips(first, own, near, far):
    above = jnp.where(first, far, near)
    below = jnp.where(first, near, far)
    return jnp.concatenate([above, own, below], axis=0)


def bring_kernel(ens, control, ens_o, control_o, sem):
    copies = [
        pltpu.make_async_copy(ens, ens_o, sem.at[0]),
        pltpu.make_async_copy(control, control_o, sem.at[1]),
    ]
    for copy in copies:
        copy.start()
    for copy in copies:
        copy.wait()


def start_kernel(pos, scal, control, far, near, ens, loc_o, part_o):
    scaled = []
    for m in range(2):
        loc = sweeps(strips(pos[0] == 0, control[m], near[m], far[m]), rate_of(pos, scal, m))
        loc_o[m] = loc
        scaled.append(scal[m] * loc)
    n = part_o.shape[1]
    for b in range(8):
        slot = lax.bitwise_xor(jnp.int32(b), pos[2])
        for j in range(0, n, 8):
            k = b * n + j
            part_o[slot, j : j + 8] = (
                ens[0, k : k + 8].astype(F32) * scaled[0][None]
                + ens[1, k : k + 8].astype(F32) * scaled[1][None]
            )


def tree(parts):
    while len(parts) > 1:
        parts = [p + q for p, q in zip(parts[::2], parts[1::2])]
    return parts[0]


def mid_kernel(parts, edge_o, inner_o):
    half = edge_o.shape[0]
    low = lax.broadcasted_iota(jnp.int32, edge_o.shape[1:], 0) < 4
    for p in range(half):
        one, two = (pltpu.roll(tree([parts[b, k] for b in range(8)]), 2, 0) for k in (p, p + half))
        edge_o[p] = jnp.where(low, one, pltpu.roll(two, 4, 0))
        inner_o[p] = jnp.where(low, pltpu.roll(one, 4, 0), two)


def edge_kernel(pos, coef, keep, got, seen, obsw, edge_o, far_o, near_o, rows):
    first = pos[0] == 0
    n = seen.shape[0]
    half = n // 2
    for p in range(half):
        edge = keep[p] + got[p]
        edge_o[p] = edge
        for j in range(4):
            row = (j + 2) % 4
            rows[row, p : p + 1] = edge[j : j + 1]
            rows[row, half + p : half + p + 1] = edge[j + 4 : j + 5]
    for p in range(n):
        rows[4, p : p + 1] = seen[p, 0:1]
        rows[5, p : p + 1] = seen[p, 7:8]
    a, b, e = coef[:, 0:1], coef[:, 1:2], coef[:, 2:3]

    def without(center, beside, sign, weight, see):
        north, south = y_pair(center)
        forward = (
            center
            - sign * a * (beside * 0.5)
            - b * ((north - south) * 0.5)
            + e * (beside + north + south - 4.0 * center)
        )
        return weight * (forward - see)

    head = (rows[0], without(rows[0], rows[1], 1.0, obsw[0:1], rows[4]), obsw[0:1])
    tail = (rows[3], without(rows[3], rows[2], -1.0, obsw[7:8], rows[5]), obsw[7:8])
    for j, (lo, hi) in enumerate(((0, n), (n, 2 * n), (2 * n, 2 * n + 1))):
        near_o[lo:hi] = jnp.where(first, tail[j], head[j])
        far_o[lo:hi] = jnp.where(first, head[j], tail[j])


def dynamics_kernel(pos, advect, damping, edge, inner, got, far, near, seen, obsw, out, above, below, inc):
    n = seen.shape[0]
    half = n // 2
    low = lax.broadcasted_iota(jnp.int32, edge.shape[1:], 0) < 4
    for p in range(half):
        outer, middle = edge[p], inner[p] + got[p]
        inc[p] = pltpu.roll(jnp.where(low, outer, pltpu.roll(middle, 4, 0)), 6, 0)
        inc[half + p] = pltpu.roll(jnp.where(low, pltpu.roll(outer, 4, 0), middle), 6, 0)
    first = pos[0] == 0
    above[...] = jnp.where(first, far[...], near[...])
    below[...] = jnp.where(first, near[...], far[...])
    weight = obsw[...]
    row = lax.broadcasted_iota(jnp.int32, weight.shape, 0)
    top, bottom = row == 0, row == weight.shape[0] - 1
    weight_above = jnp.broadcast_to(above[2 * n : 2 * n + 1], weight.shape)
    weight_below = jnp.broadcast_to(below[2 * n : 2 * n + 1], weight.shape)

    def pairs(field, over, under):
        east = jnp.where(bottom, under, pltpu.roll(field, field.shape[0] - 1, 0))
        west = jnp.where(top, over, pltpu.roll(field, 1, 0))
        north, south = y_pair(field)
        return east, west, north, south

    for p in range(n):
        k = pos[1] * n + p
        ax, ay, e = advect[0, k], advect[1, k], damping[k]
        center = inc[p]
        east, west, north, south = pairs(center, above[p : p + 1], below[p : p + 1])
        forward = (
            center
            - ax * ((east - west) * 0.5)
            - ay * ((north - south) * 0.5)
            + e * (east + west + north + south - 4.0 * center)
        )
        misfit = weight * (forward - seen[p])
        over = above[n + p : n + p + 1] + weight_above * ((e - 0.5 * ax) * center)
        under = below[n + p : n + p + 1] + weight_below * ((e + 0.5 * ax) * center)
        east, west, north, south = pairs(misfit, over, under)
        grad = (
            misfit
            + ax * ((east - west) * 0.5)
            + ay * ((north - south) * 0.5)
            + e * (east + west + north + south - 4.0 * misfit)
        )
        for b in range(8):
            out[b, p] = grad


def project_kernel(pos, scal, grad, ens, loc, send_o, sums_o):
    n = grad.shape[1]
    for m in range(2):
        parts = []
        for slot in range(8):
            first = lax.bitwise_xor(jnp.int32(slot), pos[2]) * n
            for j in range(0, n, 8):
                parts.append(
                    jnp.sum(
                        ens[m, pl.ds(first + j, 8)].astype(F32) * grad[slot, j : j + 8], axis=0
                    )
                )
            parts = [tree(parts[:4]), *parts[4:]] if slot == 0 else [parts[0] + tree(parts[1:])]
        total = parts[0]
        send_o[m] = scal[m] * total
        cells = jnp.sum(loc[m] * total, axis=0, keepdims=True)
        cells = cells[:, :128] + cells[:, 128:]
        sums_o[:, m : m + 1] = jnp.broadcast_to(cells[None], (32, 1, 128))


def end_kernel(scale, pos, scal, control, send, near, far, sums, out_o, weight_o):
    for m in range(2):
        out_o[m] = control[m] + sweeps(
            strips(pos[0] == 0, send[m], near[m], far[m]), rate_of(pos, scal, m)
        )
    total = jnp.sum(sums[...], axis=0)
    for m in range(2):
        weight_o[m] = jnp.sum(total[m : m + 1]) * scale


def swap_tiles(near, far):
    n = 32
    far_pairs = [(i, (i + 1) % n if i % 2 else (i - 1) % n) for i in range(n)]
    far = lax.ppermute(far, TILE, far_pairs)
    near = lax.ppermute(near, TILE, [(i, i ^ 1) for i in range(n)])
    return near, far


def per_device(
    ensemble, control, weights, member_band, spread, advect, damping, innovation, obs_weight
):
    n = ensemble.shape[1] // 8
    ix, zp, zq, core = (lax.axis_index(a) for a in ("x", "zp", "zq", "core"))
    own = ix * 2 + lax.bitwise_xor(zp, zq)
    pos = jnp.concatenate([jnp.stack([core, own, zp]).astype(jnp.int32), member_band])
    scal = jnp.concatenate([weights, spread])
    strip2, planes, rows = (2, 8, 256), (n, 8, 256), (2 * n + 1, 256)
    w2, wn, w4, row_spec = whole(strip2), whole(planes), whole((4, 8, 256)), whole(rows)
    strip_spec = whole((8, 256))

    hbm = pl.BlockSpec(memory_space=pltpu.HBM)
    vmem = pl.BlockSpec(memory_space=pltpu.VMEM)
    ens, own_control = pl.pallas_call(
        bring_kernel,
        in_specs=[hbm, hbm],
        out_specs=[vmem, vmem],
        out_shape=[jax.ShapeDtypeStruct(a.shape, a.dtype) for a in (ensemble, control)],
        scratch_shapes=[pltpu.SemaphoreType.DMA((2,))],
        compiler_params=pltpu.CompilerParams(vmem_limit_bytes=40 * 2**20),
        name="bring",
    )(ensemble, control)
    near0, far0 = swap_tiles(control, control)
    loc, parts = call(
        start_kernel, "start", (1,),
        [(pos, smem()), (scal, smem()), (own_control, w2), (far0, w2), (near0, w2), (ens, whole(ens.shape))],
        [(strip2, w2), ((8, n, 8, 256), whole((8, n, 8, 256)))],
    )
    parts, offset = lax.optimization_barrier((parts, (own * n).astype(jnp.uint32)))
    parts = lax.all_to_all(parts, GROUP, 0, 0, tiled=True)
    halves, wh = (n // 2, 8, 256), whole((n // 2, 8, 256))
    edge, inner = call(
        mid_kernel, "mid", (1,), [(parts, whole(parts.shape))], [(halves, wh), (halves, wh)]
    )
    across = [(0, 3), (3, 0), (1, 2), (2, 1)]
    got_edge = lax.ppermute(edge, ("zp", "zq"), across)
    got_inner = lax.ppermute(inner, ("zp", "zq"), across)
    zero = jnp.uint32(0)
    seen = lax.dynamic_slice(innovation, (offset, zero, zero), planes)
    coef = lax.dynamic_slice(jnp.concatenate([advect, damping[None]]), (zero, offset), (3, n)).T
    edge, far, near = call(
        edge_kernel, "edge", (1,),
        [(pos, smem()), (coef, whole((n, 3))), (edge, wh), (got_edge, wh), (seen, wn), (obs_weight, strip_spec)],
        [(halves, wh), (rows, row_spec), (rows, row_spec)],
        [pltpu.VMEM((6, n, 256), F32)],
    )
    near, far = swap_tiles(near, far)
    (grad,) = call(
        dynamics_kernel, "dynamics", (1,),
        [(pos, smem()), (advect, smem()), (damping, smem()), (edge, wh), (inner, wh),
         (got_inner, wh), (far, row_spec), (near, row_spec), (seen, wn), (obs_weight, strip_spec)],
        [((8, n, 8, 256), whole((8, n, 8, 256)))],
        [pltpu.VMEM(rows, F32)] * 2 + [pltpu.VMEM(planes, F32)],
    )
    grad = lax.all_to_all(grad, GROUP, 0, 0, tiled=True)
    send, sums = call(
        project_kernel, "project", (1,),
        [(pos, smem()), (scal, smem()), (grad, whole(grad.shape)),
         (ensemble, whole(ensemble.shape)), (loc, w2)],
        [(strip2, w2), ((32, 2, 128), whole((32, 2, 128)))],
    )
    near, far = swap_tiles(send, send)
    sums = lax.all_to_all(sums, TILE, 0, 0, tiled=True)
    cells = 32 * control.shape[1] * control.shape[2] * ensemble.shape[1]
    return tuple(
        call(
            functools.partial(end_kernel, 1.0 / math.sqrt(cells)), "end", (1,),
            [(pos, smem()), (scal, smem()), (control, w2), (send, w2), (near, w2), (far, w2),
             (sums, whole(sums.shape))],
            [(strip2, w2), ((2,), smem())],
        )
    )


def solution(mesh):
    mesh = Mesh(mesh.devices.reshape(4, 2, 2, 4, 4, 2), AXES)
    in_specs = (
        P(MEM, None, TILE, None),
        P(MEM, TILE, None),
        P(MEM),
        P(MEM),
        P(),
        P(),
        P(),
        P(None, TILE, None),
        P(TILE, None),
    )
    out_specs = (P(MEM, TILE, None), P(MEM))
    return jax.shard_map(
        per_device, mesh=mesh, in_specs=in_specs, out_specs=out_specs, check_vma=False
    )
```

time: 141 us -> 137 us (0.972)
  starting transfers between devices: 52.1 us -> 62.3 us
  waiting for transfers between devices: 13.7 us -> 5.04 us
  blocking collectives: 60.8 us -> 56.3 us
    ppermute x1 -> x2, waiting for transfers between devices: 7.29 us -> 0.29 us  [the longest x1 0.29 us: per_device(): got_edge = lax.ppermute(edge, ('zp', 'zq'), across)]
    all_to_all x1, starting transfers between devices: 11.6 us -> 17.8 us  [per_device(): sums = lax.all_to_all(sums, TILE, 0, 0, tiled=True)]
    all_to_all x1, blocking collectives: 29.7 us -> 25.3 us  [per_device(): grad = lax.all_to_all(grad, GROUP, 0, 0, tiled=True)]
    ppermute x1 -> x2, starting transfers between devices: 3.12 us -> 7.07 us  [the longest x1 3.95 us: per_device(): got_inner = lax.ppermute(inner, ('zp', 'zq'), across)]
    ppermute x3, waiting for transfers between devices: 3.68 us -> 2 us  [swap_tiles(): far = lax.ppermute(far, TILE, far_pairs)]
  transfers between devices with their start and end apart: 8 -> 9, of which waited for: 4 -> 4; matrix products, arithmetic and copies ran while one was open for 1% -> 1% of each run, Pallas kernels for 0% -> 1%
where the time goes in v3:
time: 137 us; the launch traced here: 136 us
  starting transfers between devices  62.3 us (45%)
  blocking collectives  56.3 us (41%)
  Pallas kernels  7.97 us (6%)
  waiting for transfers between devices  5.04 us (4%)
  local copies, waits for them, and re-layouts  2.46 us (2%)
  other arithmetic  1.56 us (1%)
    all_to_all x1, blocking collectives, per_device(): parts = lax.all_to_all(parts, GROUP, 0, 0, tiled=True)  31 us
    all_to_all x1, blocking collectives, per_device(): grad = lax.all_to_all(grad, GROUP, 0, 0, tiled=True)  25.3 us
    ppermute x3, starting transfers between devices, swap_tiles(): far = lax.ppermute(far, TILE, far_pairs)  23.4 us
    all_to_all x1, starting transfers between devices, per_device(): sums = lax.all_to_all(sums, TILE, 0, 0, tiled=True)  17.8 us
    ppermute x3, starting transfers between devices, swap_tiles(): near = lax.ppermute(near, TILE, [(i, i ^ 1) for i in range(n)])  14 us
    pallas_call x6, Pallas kernels, call(): pl.pallas_call(body, grid=grid, in_specs=[s for _, s in ins], out_specs=[...  7.79 us
    ppermute x1, starting transfers between devices, per_device(): got_inner = lax.ppermute(inner, ('zp', 'zq'), across)  3.95 us
    ppermute x1, starting transfers between devices, per_device(): got_edge = lax.ppermute(edge, ('zp', 'zq'), across)  3.12 us
  transfers between devices with their start and end apart: 9, of which 4 were waited for; matrix products, arithmetic and copies ran while one was open for 1% of the time, Pallas kernels for 1%

profile of v3, /device:TPU:1, one launch (start us, length us, event | category | flops | bytes accessed | tf_op | source)
XLA Modules:
  0.0 136.5 jit_solution(6097897365482684198)
XLA Ops:
  0.6 0.0 copy-start
  0.6 10.3 %collective-permute-start = (f32[2,8,256]{2,1,0:T(8,128)}, f32[2,8,256]{2,1,0:T(8,128)S(1)}, u32[]{:S(2)}, u32[]{:S(2)}) collective-permute-start(f32[2,8,256]{2,1,0:T(8,128)} %control.3), channel_id=1, source_target_pairs={{0,31},{1,2},{2,1},{3,4},{4,3},{5,6},{6,5},{7,8},{8,7},{9,10},{10,... | collective-permute-start | bytes 49160 | tf_op jit(solution)/shard_map/ppermute | solution.py:229
  11.0 7.8 %collective-permute-start.1 = (f32[2,8,256]{2,1,0:T(8,128)}, f32[2,8,256]{2,1,0:T(8,128)S(1)}, u32[]{:S(2)}, u32[]{:S(2)}) collective-permute-start(f32[2,8,256]{2,1,0:T(8,128)} %control.3), channel_id=1, source_target_pairs={{0,1},{1,0},{2,3},{3,2},{4,5},{5,4},{6,7},{7,6},{8,9},{9,8},{10,11... | collective-permute-start | bytes 49160 | tf_op jit(solution)/shard_map/ppermute | solution.py:230
  18.8 0.7 pad_maximum_fusion.scal
  19.6 0.7 pad_add_fusion.pos
  20.3 1.6 %copy-done.1 = bf16[2,256,8,256]{3,2,1,0:T(8,128)(2,1)S(1)} copy-done((bf16[2,256,8,256]{3,2,1,0:T(8,128)(2,1)S(1)}, bf16[2,256,8,256]{3,2,1,0:T(8,128)(2,1)}, u32[]{:S(2)}) %copy-start.1) | copy-done | bytes 2097176
  21.9 0.7 copy-done.3
  22.6 0.2 bring.1
  22.8 0.0 collective-permute-done.1.near
  22.8 1.6 %start.1 = (f32[2,8,256]{2,1,0:T(8,128)S(1)}, f32[8,32,8,256]{3,2,1,0:T(8,128)S(1)}) custom-call(s32[5]{0:T(128)S(1)} %pad_add_fusion.pos, f32[6]{0:T(128)S(1)} %pad_maximum_fusion.scal, f32[2,8,256]{2,1,0:T(8,128)S(1)} %get-tuple-element.15.control, f32[2,8,256]{2,1,0:T(8,128)S(1)} %collective-permute-done.far, ...), custom_call_target="tpu_custom_call" | custom-call | tf_op jit(solution)/shard_map/start/pallas_call | solution.py:29
  24.5 31.0 %all_to_all.15.parts = f32[8,32,8,256]{3,2,1,0:T(8,128)S(1)} all-to-all(f32[8,32,8,256]{3,2,1,0:T(8,128)S(1)} %get-tuple-element.19), channel_id=1, replica_groups=mesh['x'=4,'zp'=2,'zq'=2,'y'=4,'zh'=4,'core'=2] {'x','zq'}, dimensions={0} | all-to-all | bytes 4194304 | tf_op jit(solution)/shard_map/all_to_all | solution.py:264
  55.5 0.1 mid.1
  55.6 3.1 %collective-permute-start.2 = (f32[16,8,256]{2,1,0:T(8,128)S(1)}, f32[16,8,256]{2,1,0:T(8,128)S(1)}, u32[]{:S(2)}, u32[]{:S(2)}) collective-permute-start(f32[16,8,256]{2,1,0:T(8,128)S(1)} %get-tuple-element.20.keep), channel_id=1, source_target_pairs={{0,96},{96,0},{32,64},{64,32},{1,97},{97,1},{33,65},{65,33},{2,98}... | collective-permute-start | bytes 393224 | tf_op jit(solution)/shard_map/ppermute | solution.py:270
  58.8 0.1 fusion
  58.9 0.1 copy.15
  59.0 4.0 %collective-permute-start.3 = (f32[16,8,256]{2,1,0:T(8,128)S(1)}, f32[16,8,256]{2,1,0:T(8,128)S(1)}, u32[]{:S(2)}, u32[]{:S(2)}) collective-permute-start(f32[16,8,256]{2,1,0:T(8,128)S(1)} %get-tuple-element.22.inner), channel_id=1, source_target_pairs={{0,96},{96,0},{32,64},{64,32},{1,97},{97,1},{33,65},{65,33},{2,98}... | collective-permute-start | bytes 393224 | tf_op jit(solution)/shard_map/ppermute | solution.py:271
  63.0 0.3 collective-permute-done.2.got
  63.2 0.7 edge.1
  64.0 5.6 %collective-permute-start.4 = (f32[65,256]{1,0:T(8,128)S(1)}, f32[65,256]{1,0:T(8,128)S(1)}, u32[]{:S(2)}, u32[]{:S(2)}) collective-permute-start(f32[65,256]{1,0:T(8,128)S(1)} %get-tuple-element.23), channel_id=1, source_target_pairs={{0,31},{1,2},{2,1},{3,4},{4,3},{5,6},{6,5},{7,8},{8,7},{9,10},{10,... | collective-permute-start | bytes 199688 | tf_op jit(solution)/shard_map/ppermute | solution.py:229
  69.6 1.9 %collective-permute-start.5 = (f32[65,256]{1,0:T(8,128)S(1)}, f32[65,256]{1,0:T(8,128)S(1)}, u32[]{:S(2)}, u32[]{:S(2)}) collective-permute-start(f32[65,256]{1,0:T(8,128)S(1)} %get-tuple-element.24), channel_id=1, source_target_pairs={{0,1},{1,0},{2,3},{3,2},{4,5},{5,4},{6,7},{7,6},{8,9},{9,8},{10,11... | collective-permute-start | bytes 199688 | tf_op jit(solution)/shard_map/ppermute | solution.py:230
  71.5 0.0 collective-permute-done.3.got
  71.5 2.0 %collective-permute-done.4.far = f32[65,256]{1,0:T(8,128)S(1)} collective-permute-done((f32[65,256]{1,0:T(8,128)S(1)}, f32[65,256]{1,0:T(8,128)S(1)}, u32[]{:S(2)}, u32[]{:S(2)}) %collective-permute-start.4) | collective-permute-done | bytes 66592 | tf_op jit(solution)/shard_map/ppermute | solution.py:229
  73.5 1.9 %dynamics.1 = f32[8,32,8,256]{3,2,1,0:T(8,128)S(1)} custom-call(s32[5]{0:T(128)S(1)} %pad_add_fusion.pos, f32[2,256]{1,0:T(2,128)S(1)} %copy-done.6, f32[256]{0:T(256)S(1)} %copy-done.7, f32[16,8,256]{2,1,0:T(8,128)S(1)} %get-tuple-element.21.edge, f32[16,8,256]{2,1,0:T(8,128)S(1)} %get-tuple-element.22.inner, f32[16,8,256]{2,1,0:T(8,128)S(1)} %collective-permute-done.3.got, ...), custom_call_target="tpu_custom_call" | custom-call | tf_op jit(solution)/shard_map/dynamics/pallas_call | solution.py:29
  75.5 0.0 copy-start.2
  75.5 25.3 %all_to_all.16.grad = f32[8,32,8,256]{3,2,1,0:T(8,128)S(1)} all-to-all(f32[8,32,8,256]{3,2,1,0:T(8,128)S(1)} %dynamics.1), channel_id=1, replica_groups=mesh['x'=4,'zp'=2,'zq'=2,'y'=4,'zh'=4,'core'=2] {'x','zq'}, dimensions={0} | all-to-all | bytes 4194304 | tf_op jit(solution)/shard_map/all_to_all | solution.py:289
  100.8 1.7 %project.1 = (f32[2,8,256]{2,1,0:T(8,128)S(1)}, f32[32,2,128]{2,1,0:T(2,128)}) custom-call(s32[5]{0:T(128)S(1)} %pad_add_fusion.pos, f32[6]{0:T(128)S(1)} %pad_maximum_fusion.scal, f32[8,32,8,256]{3,2,1,0:T(8,128)S(1)} %all_to_all.16.grad, bf16[2,256,8,256]{3,2,1,0:T(8,128)(2,1)S(1)} %copy-done.2, f32[2,8,256]{2,1,0:T(8,128)S(1)} %get-tuple-element.25.loc), custom_call_target="tpu_custom_call" | custom-call | tf_op jit(solution)/shard_map/project/pallas_call | solution.py:29
  102.4 17.8 %all-to-all-start.2 = ((f32[32,2,128]{2,1,0:T(2,128)}), f32[32,2,128]{2,1,0:T(2,128)S(1)}, u32[]{:S(2)}, u32[]{:S(2)}) async-start(f32[32,2,128]{2,1,0:T(2,128)} %get-tuple-element.27), calls=%async_computation.2 | async-start | bytes 65536 | tf_op jit(solution)/shard_map/all_to_all | solution.py:297
  120.2 7.4 %collective-permute-start.7 = (f32[2,8,256]{2,1,0:T(8,128)S(1)}, f32[2,8,256]{2,1,0:T(8,128)S(1)}, u32[]{:S(2)}, u32[]{:S(2)}) collective-permute-start(f32[2,8,256]{2,1,0:T(8,128)S(1)} %get-tuple-element.26.send), channel_id=1, source_target_pairs={{0,31},{1,2},{2,1},{3,4},{4,3},{5,6},{6,5},{7,8},{8,7},{9,10},{10,... | collective-permute-start | bytes 49160 | tf_op jit(solution)/shard_map/ppermute | solution.py:229
  127.7 4.3 %collective-permute-start.6 = (f32[2,8,256]{2,1,0:T(8,128)S(1)}, f32[2,8,256]{2,1,0:T(8,128)S(1)}, u32[]{:S(2)}, u32[]{:S(2)}) collective-permute-start(f32[2,8,256]{2,1,0:T(8,128)S(1)} %get-tuple-element.26.send), channel_id=1, source_target_pairs={{0,1},{1,0},{2,3},{3,2},{4,5},{5,4},{6,7},{7,6},{8,9},{9,8},{10,11... | collective-permute-start | bytes 49160 | tf_op jit(solution)/shard_map/ppermute | solution.py:230
  132.0 0.8 collective-permute-done.6.near
  132.8 1.9 %all-to-all-done.2.sums = f32[32,2,128]{2,1,0:T(2,128)S(1)} async-done(((f32[32,2,128]{2,1,0:T(2,128)}), f32[32,2,128]{2,1,0:T(2,128)S(1)}, u32[]{:S(2)}, u32[]{:S(2)}) %all-to-all-start.2) | async-done | bytes 32800 | tf_op jit(solution)/shard_map/all_to_all | solution.py:297
  134.7 1.8 %end.1 = (f32[2,8,256]{2,1,0:T(8,128)}, f32[2]{0:T(128)}) custom-call(s32[5]{0:T(128)S(1)} %pad_add_fusion.pos, f32[6]{0:T(128)S(1)} %pad_maximum_fusion.scal, f32[2,8,256]{2,1,0:T(8,128)S(1)} %copy-done.4, f32[2,8,256]{2,1,0:T(8,128)S(1)} %get-tuple-element.26.send, f32[2,8,256]{2,1,0:T(8,128)S(1)} %collective-permute-done.6.near, ...), custom_call_target="tpu_custom_call" | custom-call | tf_op jit(solution)/shard_map/end/pallas_call | solution.py:29
  (16 shorter events, 0.1 us)
Async XLA Ops:
  0.6 62.3 %copy-start = (f32[256,8,256]{2,1,0:T(8,128)S(1)}, f32[256,8,256]{2,1,0:T(8,128)}, u32[]{:S(2)}) copy-start(f32[256,8,256]{2,1,0:T(8,128)} %param.16) | copy-start | bytes 6291460
  0.6 22.2 %collective-permute-start = (f32[2,8,256]{2,1,0:T(8,128)}, f32[2,8,256]{2,1,0:T(8,128)S(1)}, u32[]{:S(2)}, u32[]{:S(2)}) collective-permute-start(f32[2,8,256]{2,1,0:T(8,128)} %control.3), channel_id=1, source_target_pairs={{0,31},{1,2},{2,1},{3,4},{4,3},{5,6},{6,5},{7,8},{8,7},{9,10},{10,... | collective-permute-start | bytes 49160 | tf_op jit(solution)/shard_map/ppermute | solution.py:229
  11.0 11.8 %collective-permute-start.1 = (f32[2,8,256]{2,1,0:T(8,128)}, f32[2,8,256]{2,1,0:T(8,128)S(1)}, u32[]{:S(2)}, u32[]{:S(2)}) collective-permute-start(f32[2,8,256]{2,1,0:T(8,128)} %control.3), channel_id=1, source_target_pairs={{0,1},{1,0},{2,3},{3,2},{4,5},{5,4},{6,7},{7,6},{8,9},{9,8},{10,11... | collective-permute-start | bytes 49160 | tf_op jit(solution)/shard_map/ppermute | solution.py:230
  20.3 1.6 %copy-start.1 = (bf16[2,256,8,256]{3,2,1,0:T(8,128)(2,1)S(1)}, bf16[2,256,8,256]{3,2,1,0:T(8,128)(2,1)}, u32[]{:S(2)}) copy-start(bf16[2,256,8,256]{3,2,1,0:T(8,128)(2,1)} %ens.3) | copy-start | bytes 6291460
  21.9 0.7 copy-start.3
  55.5 3.2 %copy-start.6 = (f32[2,256]{1,0:T(2,128)S(1)}, f32[2,256]{1,0:T(2,128)}, u32[]{:S(2)}) copy-start(f32[2,256]{1,0:T(2,128)} %advect.1) | copy-start | bytes 6148
  55.5 3.2 %copy-start.7 = (f32[256]{0:T(256)S(1)}, f32[256]{0:T(256)}, u32[]{:S(2)}) copy-start(f32[256]{0:T(256)} %damping.1) | copy-start | bytes 3076
  55.5 7.7 %copy-start.5 = (f32[8,256]{1,0:T(8,128)S(1)}, f32[8,256]{1,0:T(8,128)}, u32[]{:S(2)}) copy-start(f32[8,256]{1,0:T(8,128)} %obsw.3) | copy-start | bytes 24580
  55.6 7.6 %collective-permute-start.2 = (f32[16,8,256]{2,1,0:T(8,128)S(1)}, f32[16,8,256]{2,1,0:T(8,128)S(1)}, u32[]{:S(2)}, u32[]{:S(2)}) collective-permute-start(f32[16,8,256]{2,1,0:T(8,128)S(1)} %get-tuple-element.20.keep), channel_id=1, source_target_pairs={{0,96},{96,0},{32,64},{64,32},{1,97},{97,1},{33,65},{65,33},{2,98}... | collective-permute-start | bytes 393224 | tf_op jit(solution)/shard_map/ppermute | solution.py:270
  59.0 12.6 %collective-permute-start.3 = (f32[16,8,256]{2,1,0:T(8,128)S(1)}, f32[16,8,256]{2,1,0:T(8,128)S(1)}, u32[]{:S(2)}, u32[]{:S(2)}) collective-permute-start(f32[16,8,256]{2,1,0:T(8,128)S(1)} %get-tuple-element.22.inner), channel_id=1, source_target_pairs={{0,96},{96,0},{32,64},{64,32},{1,97},{97,1},{33,65},{65,33},{2,98}... | collective-permute-start | bytes 393224 | tf_op jit(solution)/shard_map/ppermute | solution.py:271
  64.0 9.6 %collective-permute-start.4 = (f32[65,256]{1,0:T(8,128)S(1)}, f32[65,256]{1,0:T(8,128)S(1)}, u32[]{:S(2)}, u32[]{:S(2)}) collective-permute-start(f32[65,256]{1,0:T(8,128)S(1)} %get-tuple-element.23), channel_id=1, source_target_pairs={{0,31},{1,2},{2,1},{3,4},{4,3},{5,6},{6,5},{7,8},{8,7},{9,10},{10,... | collective-permute-start | bytes 199688 | tf_op jit(solution)/shard_map/ppermute | solution.py:229
  69.6 3.9 %collective-permute-start.5 = (f32[65,256]{1,0:T(8,128)S(1)}, f32[65,256]{1,0:T(8,128)S(1)}, u32[]{:S(2)}, u32[]{:S(2)}) collective-permute-start(f32[65,256]{1,0:T(8,128)S(1)} %get-tuple-element.24), channel_id=1, source_target_pairs={{0,1},{1,0},{2,3},{3,2},{4,5},{5,4},{6,7},{7,6},{8,9},{9,8},{10,11... | collective-permute-start | bytes 199688 | tf_op jit(solution)/shard_map/ppermute | solution.py:230
  75.5 25.3 %copy-start.2 = (bf16[2,256,8,256]{3,2,1,0:T(8,128)(2,1)S(1)}, bf16[2,256,8,256]{3,2,1,0:T(8,128)(2,1)}, u32[]{:S(2)}) copy-start(bf16[2,256,8,256]{3,2,1,0:T(8,128)(2,1)} %ens.3) | copy-start | bytes 6291460
  100.8 33.9 %copy-start.4 = (f32[2,8,256]{2,1,0:T(8,128)S(1)}, f32[2,8,256]{2,1,0:T(8,128)}, u32[]{:S(2)}) copy-start(f32[2,8,256]{2,1,0:T(8,128)} %control.3) | copy-start | bytes 49156
  102.4 32.3 %all-to-all-start.2 = ((f32[32,2,128]{2,1,0:T(2,128)}), f32[32,2,128]{2,1,0:T(2,128)S(1)}, u32[]{:S(2)}, u32[]{:S(2)}) async-start(f32[32,2,128]{2,1,0:T(2,128)} %get-tuple-element.27), calls=%async_computation.2 | async-start | bytes 65536 | tf_op jit(solution)/shard_map/all_to_all | solution.py:297
  120.2 11.7 %collective-permute-start.7 = (f32[2,8,256]{2,1,0:T(8,128)S(1)}, f32[2,8,256]{2,1,0:T(8,128)S(1)}, u32[]{:S(2)}, u32[]{:S(2)}) collective-permute-start(f32[2,8,256]{2,1,0:T(8,128)S(1)} %get-tuple-element.26.send), channel_id=1, source_target_pairs={{0,31},{1,2},{2,1},{3,4},{4,3},{5,6},{6,5},{7,8},{8,7},{9,10},{10,... | collective-permute-start | bytes 49160 | tf_op jit(solution)/shard_map/ppermute | solution.py:229
  127.7 5.1 %collective-permute-start.6 = (f32[2,8,256]{2,1,0:T(8,128)S(1)}, f32[2,8,256]{2,1,0:T(8,128)S(1)}, u32[]{:S(2)}, u32[]{:S(2)}) collective-permute-start(f32[2,8,256]{2,1,0:T(8,128)S(1)} %get-tuple-element.26.send), channel_id=1, source_target_pairs={{0,1},{1,0},{2,3},{3,2},{4,5},{5,4},{6,7},{7,6},{8,9},{9,8},{10,11... | collective-permute-start | bytes 49160 | tf_op jit(solution)/shard_map/ppermute | solution.py:230

commit v4 on v3

--- a/solution.py
+++ b/solution.py
@@ -12,7 +12,7 @@
 SWEEPS = 8
 AXES = ("x", "zp", "zq", "y", "zh", "core")
 MEM = ("x", "zp", "zq")
-GROUP = ("x", "zq")
+GROUP = ("zq", "x")
 TILE = ("y", "zh", "core")
 F32 = jnp.float32
 
@@ -25,17 +25,18 @@
     return pl.BlockSpec(shape, lambda *i: (0,) * len(shape))
 
 
-def call(body, name, grid, ins, outs, scratch=(), vmem=40 * 2**20):
+def call(body, name, ins, outs, scratch=(), results=None):
+    scalars, arrays = ins
+    vmem = pl.BlockSpec(memory_space=pltpu.VMEM)
     return pl.pallas_call(
         body,
-        grid=grid,
-        in_specs=[s for _, s in ins],
-        out_specs=[s for _, s in outs],
-        out_shape=[jax.ShapeDtypeStruct(shape, F32) for shape, _ in outs],
+        in_specs=[smem() for _ in scalars] + [vmem for _ in arrays],
+        out_specs=results if results else [vmem for _ in outs],
+        out_shape=[jax.ShapeDtypeStruct(shape, F32) for shape in outs],
         scratch_shapes=list(scratch),
-        compiler_params=pltpu.CompilerParams(vmem_limit_bytes=vmem),
+        compiler_params=pltpu.CompilerParams(vmem_limit_bytes=40 * 2**20),
         name=name,
-    )(*[a for a, _ in ins])
+    )(*scalars, *arrays)
 
 
 def y_pair(field):
@@ -195,20 +196,17 @@
 
 def project_kernel(pos, scal, grad, ens, loc, send_o, sums_o):
     n = grad.shape[1]
+    totals = [None, None]
+    for slot in range(8):
+        first = lax.bitwise_xor(jnp.int32(slot), pos[2]) * n
+        for j in range(0, n, 4):
+            part = grad[slot, j : j + 4]
+            for m in range(2):
+                more = tree([ens[m, first + j + i].astype(F32) * part[i] for i in range(4)])
+                totals[m] = more if totals[m] is None else totals[m] + more
     for m in range(2):
-        parts = []
-        for slot in range(8):
-            first = lax.bitwise_xor(jnp.int32(slot), pos[2]) * n
-            for j in range(0, n, 8):
-                parts.append(
-                    jnp.sum(
-                        ens[m, pl.ds(first + j, 8)].astype(F32) * grad[slot, j : j + 8], axis=0
-                    )
-                )
-            parts = [tree(parts[:4]), *parts[4:]] if slot == 0 else [parts[0] + tree(parts[1:])]
-        total = parts[0]
-        send_o[m] = scal[m] * total
-        cells = jnp.sum(loc[m] * total, axis=0, keepdims=True)
+        send_o[m] = scal[m] * totals[m]
+        cells = jnp.sum(loc[m] * totals[m], axis=0, keepdims=True)
         cells = cells[:, :128] + cells[:, 128:]
         sums_o[:, m : m + 1] = jnp.broadcast_to(cells[None], (32, 1, 128))
 
@@ -236,12 +234,11 @@
 ):
     n = ensemble.shape[1] // 8
     ix, zp, zq, core = (lax.axis_index(a) for a in ("x", "zp", "zq", "core"))
-    own = ix * 2 + lax.bitwise_xor(zp, zq)
-    pos = jnp.concatenate([jnp.stack([core, own, zp]).astype(jnp.int32), member_band])
+    own = lax.bitwise_xor(zp, zq) * 4 + ix
+    pos = jnp.concatenate([jnp.stack([core, own, zp * 4]).astype(jnp.int32), member_band])
     scal = jnp.concatenate([weights, spread])
     strip2, planes, rows = (2, 8, 256), (n, 8, 256), (2 * n + 1, 256)
-    w2, wn, w4, row_spec = whole(strip2), whole(planes), whole((4, 8, 256)), whole(rows)
-    strip_spec = whole((8, 256))
+    halves, blocks = (n // 2, 8, 256), (8, n, 8, 256)
 
     hbm = pl.BlockSpec(memory_space=pltpu.HBM)
     vmem = pl.BlockSpec(memory_space=pltpu.VMEM)
@@ -256,16 +253,11 @@
     )(ensemble, control)
     near0, far0 = swap_tiles(control, control)
     loc, parts = call(
-        start_kernel, "start", (1,),
-        [(pos, smem()), (scal, smem()), (own_control, w2), (far0, w2), (near0, w2), (ens, whole(ens.shape))],
-        [(strip2, w2), ((8, n, 8, 256), whole((8, n, 8, 256)))],
+        start_kernel, "start", ([pos, scal], [own_control, far0, near0, ens]), [strip2, blocks]
     )
     parts, offset = lax.optimization_barrier((parts, (own * n).astype(jnp.uint32)))
     parts = lax.all_to_all(parts, GROUP, 0, 0, tiled=True)
-    halves, wh = (n // 2, 8, 256), whole((n // 2, 8, 256))
-    edge, inner = call(
-        mid_kernel, "mid", (1,), [(parts, whole(parts.shape))], [(halves, wh), (halves, wh)]
-    )
+    edge, inner = call(mid_kernel, "mid", ([], [parts]), [halves, halves])
     across = [(0, 3), (3, 0), (1, 2), (2, 1)]
     got_edge = lax.ppermute(edge, ("zp", "zq"), across)
     got_inner = lax.ppermute(inner, ("zp", "zq"), across)
@@ -273,36 +265,32 @@
     seen = lax.dynamic_slice(innovation, (offset, zero, zero), planes)
     coef = lax.dynamic_slice(jnp.concatenate([advect, damping[None]]), (zero, offset), (3, n)).T
     edge, far, near = call(
-        edge_kernel, "edge", (1,),
-        [(pos, smem()), (coef, whole((n, 3))), (edge, wh), (got_edge, wh), (seen, wn), (obs_weight, strip_spec)],
-        [(halves, wh), (rows, row_spec), (rows, row_spec)],
-        [pltpu.VMEM((6, n, 256), F32)],
+        edge_kernel, "edge", ([pos], [coef, edge, got_edge, seen, obs_weight]),
+        [halves, rows, rows], [pltpu.VMEM((6, n, 256), F32)],
     )
     near, far = swap_tiles(near, far)
     (grad,) = call(
-        dynamics_kernel, "dynamics", (1,),
-        [(pos, smem()), (advect, smem()), (damping, smem()), (edge, wh), (inner, wh),
-         (got_inner, wh), (far, row_spec), (near, row_spec), (seen, wn), (obs_weight, strip_spec)],
-        [((8, n, 8, 256), whole((8, n, 8, 256)))],
-        [pltpu.VMEM(rows, F32)] * 2 + [pltpu.VMEM(planes, F32)],
+        dynamics_kernel, "dynamics",
+        ([pos, advect, damping], [edge, inner, got_inner, far, near, seen, obs_weight]),
+        [blocks], [pltpu.VMEM(rows, F32)] * 2 + [pltpu.VMEM(planes, F32)],
     )
     grad = lax.all_to_all(grad, GROUP, 0, 0, tiled=True)
     send, sums = call(
-        project_kernel, "project", (1,),
-        [(pos, smem()), (scal, smem()), (grad, whole(grad.shape)),
-         (ensemble, whole(ensemble.shape)), (loc, w2)],
-        [(strip2, w2), ((32, 2, 128), whole((32, 2, 128)))],
+        project_kernel, "project", ([pos, scal], [grad, ensemble, loc]), [strip2, (32, 2, 128)]
     )
     near, far = swap_tiles(send, send)
     sums = lax.all_to_all(sums, TILE, 0, 0, tiled=True)
     cells = 32 * control.shape[1] * control.shape[2] * ensemble.shape[1]
     return tuple(
-        call(
-            functools.partial(end_kernel, 1.0 / math.sqrt(cells)), "end", (1,),
-            [(pos, smem()), (scal, smem()), (control, w2), (send, w2), (near, w2), (far, w2),
-             (sums, whole(sums.shape))],
-            [(strip2, w2), ((2,), smem())],
-        )
+        pl.pallas_call(
+            functools.partial(end_kernel, 1.0 / math.sqrt(cells)),
+            grid=(1,),
+            in_specs=[smem(), smem()] + [whole(strip2)] * 4 + [whole(sums.shape)],
+            out_specs=[whole(strip2), smem()],
+            out_shape=[jax.ShapeDtypeStruct(strip2, F32), jax.ShapeDtypeStruct((2,), F32)],
+            compiler_params=pltpu.CompilerParams(vmem_limit_bytes=40 * 2**20),
+            name="end",
+        )(pos, scal, control, send, near, far, sums)
     )
 
 

time: 137 us -> 137 us (level)
  blocking collectives: 56.3 us -> 60.3 us
  starting transfers between devices: 62.3 us -> 58.7 us
    all_to_all x1, starting transfers between devices: 17.8 us -> 12.5 us  [per_device(): sums = lax.all_to_all(sums, TILE, 0, 0, tiled=True)]
    all_to_all x1, blocking collectives: 25.3 us -> 30.3 us  [per_device(): grad = lax.all_to_all(grad, GROUP, 0, 0, tiled=True)]
    ppermute x3, starting transfers between devices: 23.4 us -> 25.1 us  [swap_tiles(): far = lax.ppermute(far, TILE, far_pairs)]
    ppermute x3, waiting for transfers between devices: 2 us -> 0.38 us  [swap_tiles(): far = lax.ppermute(far, TILE, far_pairs)]
  transfers between devices with their start and end apart: 9 -> 9, of which waited for: 4 -> 5; matrix products, arithmetic and copies ran while one was open for 1% -> 1% of each run, Pallas kernels for 1% -> 1%
where the time goes in v4:
time: 137 us; the launch traced here: 136 us
  blocking collectives  60.3 us (44%)
  starting transfers between devices  58.7 us (43%)
  Pallas kernels  7.95 us (6%)
  waiting for transfers between devices  4.23 us (3%)
  local copies, waits for them, and re-layouts  2.46 us (2%)
  other arithmetic  1.56 us (1%)
    all_to_all x1, blocking collectives, per_device(): grad = lax.all_to_all(grad, GROUP, 0, 0, tiled=True)  30.3 us
    all_to_all x1, blocking collectives, per_device(): parts = lax.all_to_all(parts, GROUP, 0, 0, tiled=True)  30.1 us
    ppermute x3, starting transfers between devices, swap_tiles(): far = lax.ppermute(far, TILE, far_pairs)  25.1 us
    ppermute x3, starting transfers between devices, swap_tiles(): near = lax.ppermute(near, TILE, [(i, i ^ 1) for i in range(n)])  14 us
    all_to_all x1, starting transfers between devices, per_device(): sums = lax.all_to_all(sums, TILE, 0, 0, tiled=True)  12.5 us
    pallas_call x5, Pallas kernels, call(): pl.pallas_call(body, in_specs=[smem() for _ in scalars] + [vmem for _ in...  5.99 us
    ppermute x1, starting transfers between devices, per_device(): got_inner = lax.ppermute(inner, ('zp', 'zq'), across)  3.57 us
    ppermute x1, starting transfers between devices, per_device(): got_edge = lax.ppermute(edge, ('zp', 'zq'), across)  3.5 us
  transfers between devices with their start and end apart: 9, of which 5 were waited for; matrix products, arithmetic and copies ran while one was open for 1% of the time, Pallas kernels for 1%

profile of v4, /device:TPU:1, one launch (start us, length us, event | category | flops | bytes accessed | tf_op | source)
XLA Modules:
  0.0 136.0 jit_solution(16412451166752908449)
XLA Ops:
  0.6 0.0 copy-start
  0.6 10.3 %collective-permute-start = (f32[2,8,256]{2,1,0:T(8,128)}, f32[2,8,256]{2,1,0:T(8,128)S(1)}, u32[]{:S(2)}, u32[]{:S(2)}) collective-permute-start(f32[2,8,256]{2,1,0:T(8,128)} %control.3), channel_id=1, source_target_pairs={{0,31},{1,2},{2,1},{3,4},{4,3},{5,6},{6,5},{7,8},{8,7},{9,10},{10,... | collective-permute-start | bytes 49160 | tf_op jit(solution)/shard_map/ppermute | solution.py:227
  11.0 7.8 %collective-permute-start.1 = (f32[2,8,256]{2,1,0:T(8,128)}, f32[2,8,256]{2,1,0:T(8,128)S(1)}, u32[]{:S(2)}, u32[]{:S(2)}) collective-permute-start(f32[2,8,256]{2,1,0:T(8,128)} %control.3), channel_id=1, source_target_pairs={{0,1},{1,0},{2,3},{3,2},{4,5},{5,4},{6,7},{7,6},{8,9},{9,8},{10,11... | collective-permute-start | bytes 49160 | tf_op jit(solution)/shard_map/ppermute | solution.py:228
  18.8 0.7 pad_maximum_fusion.scal
  19.6 0.7 pad_add_fusion.pos
  20.3 1.6 %copy-done.1 = bf16[2,256,8,256]{3,2,1,0:T(8,128)(2,1)S(1)} copy-done((bf16[2,256,8,256]{3,2,1,0:T(8,128)(2,1)S(1)}, bf16[2,256,8,256]{3,2,1,0:T(8,128)(2,1)}, u32[]{:S(2)}) %copy-start.1) | copy-done | bytes 2097176
  21.9 0.7 copy-done.3
  22.6 0.2 bring.1
  22.8 0.0 collective-permute-done.far
  22.8 1.6 %start.1 = (f32[2,8,256]{2,1,0:T(8,128)S(1)}, f32[8,32,8,256]{3,2,1,0:T(8,128)S(1)}) custom-call(s32[5]{0:T(128)S(1)} %pad_add_fusion.pos, f32[6]{0:T(128)S(1)} %pad_maximum_fusion.scal, f32[2,8,256]{2,1,0:T(8,128)S(1)} %get-tuple-element.15.control, f32[2,8,256]{2,1,0:T(8,128)S(1)} %collective-permute-done.far, ...), custom_call_target="tpu_custom_call" | custom-call | tf_op jit(solution)/shard_map/start/pallas_call | solution.py:31
  24.5 30.1 %all_to_all.15.parts = f32[8,32,8,256]{3,2,1,0:T(8,128)S(1)} all-to-all(f32[8,32,8,256]{3,2,1,0:T(8,128)S(1)} %get-tuple-element.19), channel_id=1, replica_groups=mesh['x'=4,'zp'=2,'zq'=2,'y'=4,'zh'=4,'core'=2] {'zq','x'}, dimensions={0} | all-to-all | bytes 4194304 | tf_op jit(solution)/shard_map/all_to_all | solution.py:259
  54.5 0.1 mid.1
  54.6 3.5 %collective-permute-start.2 = (f32[16,8,256]{2,1,0:T(8,128)S(1)}, f32[16,8,256]{2,1,0:T(8,128)S(1)}, u32[]{:S(2)}, u32[]{:S(2)}) collective-permute-start(f32[16,8,256]{2,1,0:T(8,128)S(1)} %get-tuple-element.20.keep), channel_id=1, source_target_pairs={{0,96},{96,0},{32,64},{64,32},{1,97},{97,1},{33,65},{65,33},{2,98}... | collective-permute-start | bytes 393224 | tf_op jit(solution)/shard_map/ppermute | solution.py:262
  58.2 0.1 fusion
  58.2 0.1 copy.15
  58.3 3.6 %collective-permute-start.3 = (f32[16,8,256]{2,1,0:T(8,128)S(1)}, f32[16,8,256]{2,1,0:T(8,128)S(1)}, u32[]{:S(2)}, u32[]{:S(2)}) collective-permute-start(f32[16,8,256]{2,1,0:T(8,128)S(1)} %get-tuple-element.22.inner), channel_id=1, source_target_pairs={{0,96},{96,0},{32,64},{64,32},{1,97},{97,1},{33,65},{65,33},{2,98}... | collective-permute-start | bytes 393224 | tf_op jit(solution)/shard_map/ppermute | solution.py:263
  62.0 0.3 collective-permute-done.2.got
  62.2 0.7 edge.1
  62.9 7.4 %collective-permute-start.4 = (f32[65,256]{1,0:T(8,128)S(1)}, f32[65,256]{1,0:T(8,128)S(1)}, u32[]{:S(2)}, u32[]{:S(2)}) collective-permute-start(f32[65,256]{1,0:T(8,128)S(1)} %get-tuple-element.23), channel_id=1, source_target_pairs={{0,31},{1,2},{2,1},{3,4},{4,3},{5,6},{6,5},{7,8},{8,7},{9,10},{10,... | collective-permute-start | bytes 199688 | tf_op jit(solution)/shard_map/ppermute | solution.py:227
  70.3 1.9 %collective-permute-start.5 = (f32[65,256]{1,0:T(8,128)S(1)}, f32[65,256]{1,0:T(8,128)S(1)}, u32[]{:S(2)}, u32[]{:S(2)}) collective-permute-start(f32[65,256]{1,0:T(8,128)S(1)} %get-tuple-element.24), channel_id=1, source_target_pairs={{0,1},{1,0},{2,3},{3,2},{4,5},{5,4},{6,7},{7,6},{8,9},{9,8},{10,11... | collective-permute-start | bytes 199688 | tf_op jit(solution)/shard_map/ppermute | solution.py:228
  72.2 0.4 collective-permute-done.4.far
  72.6 0.8 collective-permute-done.5.near
  73.5 1.9 %dynamics.1 = f32[8,32,8,256]{3,2,1,0:T(8,128)S(1)} custom-call(s32[5]{0:T(128)S(1)} %pad_add_fusion.pos, f32[2,256]{1,0:T(2,128)S(1)} %copy-done.6, f32[256]{0:T(256)S(1)} %copy-done.7, f32[16,8,256]{2,1,0:T(8,128)S(1)} %get-tuple-element.21.edge, f32[16,8,256]{2,1,0:T(8,128)S(1)} %get-tuple-element.22.inner, f32[16,8,256]{2,1,0:T(8,128)S(1)} %collective-permute-done.3.got, ...), custom_call_target="tpu_custom_call" | custom-call | tf_op jit(solution)/shard_map/dynamics/pallas_call | solution.py:31
  75.4 0.0 copy-start.2
  75.4 30.3 %all_to_all.16.grad = f32[8,32,8,256]{3,2,1,0:T(8,128)S(1)} all-to-all(f32[8,32,8,256]{3,2,1,0:T(8,128)S(1)} %dynamics.1), channel_id=1, replica_groups=mesh['x'=4,'zp'=2,'zq'=2,'y'=4,'zh'=4,'core'=2] {'zq','x'}, dimensions={0} | all-to-all | bytes 4194304 | tf_op jit(solution)/shard_map/all_to_all | solution.py:277
  105.7 1.6 %project.1 = (f32[2,8,256]{2,1,0:T(8,128)S(1)}, f32[32,2,128]{2,1,0:T(2,128)}) custom-call(s32[5]{0:T(128)S(1)} %pad_add_fusion.pos, f32[6]{0:T(128)S(1)} %pad_maximum_fusion.scal, f32[8,32,8,256]{3,2,1,0:T(8,128)S(1)} %all_to_all.16.grad, bf16[2,256,8,256]{3,2,1,0:T(8,128)(2,1)S(1)} %copy-done.2, f32[2,8,256]{2,1,0:T(8,128)S(1)} %get-tuple-element.25.loc), custom_call_target="tpu_custom_call" | custom-call | tf_op jit(solution)/shard_map/project/pallas_call | solution.py:31
  107.3 12.5 %all-to-all-start.2 = ((f32[32,2,128]{2,1,0:T(2,128)}), f32[32,2,128]{2,1,0:T(2,128)S(1)}, u32[]{:S(2)}, u32[]{:S(2)}) async-start(f32[32,2,128]{2,1,0:T(2,128)} %get-tuple-element.27), calls=%async_computation.2 | async-start | bytes 65536 | tf_op jit(solution)/shard_map/all_to_all | solution.py:282
  119.8 7.4 %collective-permute-start.7 = (f32[2,8,256]{2,1,0:T(8,128)S(1)}, f32[2,8,256]{2,1,0:T(8,128)S(1)}, u32[]{:S(2)}, u32[]{:S(2)}) collective-permute-start(f32[2,8,256]{2,1,0:T(8,128)S(1)} %get-tuple-element.26.send), channel_id=1, source_target_pairs={{0,31},{1,2},{2,1},{3,4},{4,3},{5,6},{6,5},{7,8},{8,7},{9,10},{10,... | collective-permute-start | bytes 49160 | tf_op jit(solution)/shard_map/ppermute | solution.py:227
  127.2 4.3 %collective-permute-start.6 = (f32[2,8,256]{2,1,0:T(8,128)S(1)}, f32[2,8,256]{2,1,0:T(8,128)S(1)}, u32[]{:S(2)}, u32[]{:S(2)}) collective-permute-start(f32[2,8,256]{2,1,0:T(8,128)S(1)} %get-tuple-element.26.send), channel_id=1, source_target_pairs={{0,1},{1,0},{2,3},{3,2},{4,5},{5,4},{6,7},{7,6},{8,9},{9,8},{10,11... | collective-permute-start | bytes 49160 | tf_op jit(solution)/shard_map/ppermute | solution.py:228
  131.5 0.8 collective-permute-done.6.near
  132.3 1.9 %all-to-all-done.2.sums = f32[32,2,128]{2,1,0:T(2,128)S(1)} async-done(((f32[32,2,128]{2,1,0:T(2,128)}), f32[32,2,128]{2,1,0:T(2,128)S(1)}, u32[]{:S(2)}, u32[]{:S(2)}) %all-to-all-start.2) | async-done | bytes 32800 | tf_op jit(solution)/shard_map/all_to_all | solution.py:282
  134.3 1.8 %end.1 = (f32[2,8,256]{2,1,0:T(8,128)}, f32[2]{0:T(128)}) custom-call(s32[5]{0:T(128)S(1)} %pad_add_fusion.pos, f32[6]{0:T(128)S(1)} %pad_maximum_fusion.scal, f32[2,8,256]{2,1,0:T(8,128)S(1)} %copy-done.4, f32[2,8,256]{2,1,0:T(8,128)S(1)} %get-tuple-element.26.send, f32[2,8,256]{2,1,0:T(8,128)S(1)} %collective-permute-done.6.near, ...), custom_call_target="tpu_custom_call" | custom-call | tf_op jit(solution)/shard_map/end/pallas_call | solution.py:285
  (16 shorter events, 0.1 us)
Async XLA Ops:
  0.6 61.3 %copy-start = (f32[256,8,256]{2,1,0:T(8,128)S(1)}, f32[256,8,256]{2,1,0:T(8,128)}, u32[]{:S(2)}) copy-start(f32[256,8,256]{2,1,0:T(8,128)} %param.16) | copy-start | bytes 6291460
  0.6 22.2 %collective-permute-start = (f32[2,8,256]{2,1,0:T(8,128)}, f32[2,8,256]{2,1,0:T(8,128)S(1)}, u32[]{:S(2)}, u32[]{:S(2)}) collective-permute-start(f32[2,8,256]{2,1,0:T(8,128)} %control.3), channel_id=1, source_target_pairs={{0,31},{1,2},{2,1},{3,4},{4,3},{5,6},{6,5},{7,8},{8,7},{9,10},{10,... | collective-permute-start | bytes 49160 | tf_op jit(solution)/shard_map/ppermute | solution.py:227
  11.0 11.8 %collective-permute-start.1 = (f32[2,8,256]{2,1,0:T(8,128)}, f32[2,8,256]{2,1,0:T(8,128)S(1)}, u32[]{:S(2)}, u32[]{:S(2)}) collective-permute-start(f32[2,8,256]{2,1,0:T(8,128)} %control.3), channel_id=1, source_target_pairs={{0,1},{1,0},{2,3},{3,2},{4,5},{5,4},{6,7},{7,6},{8,9},{9,8},{10,11... | collective-permute-start | bytes 49160 | tf_op jit(solution)/shard_map/ppermute | solution.py:228
  20.3 1.6 %copy-start.1 = (bf16[2,256,8,256]{3,2,1,0:T(8,128)(2,1)S(1)}, bf16[2,256,8,256]{3,2,1,0:T(8,128)(2,1)}, u32[]{:S(2)}) copy-start(bf16[2,256,8,256]{3,2,1,0:T(8,128)(2,1)} %ens.3) | copy-start | bytes 6291460
  21.9 0.7 copy-start.3
  54.5 3.6 %copy-start.6 = (f32[2,256]{1,0:T(2,128)S(1)}, f32[2,256]{1,0:T(2,128)}, u32[]{:S(2)}) copy-start(f32[2,256]{1,0:T(2,128)} %advect.1) | copy-start | bytes 6148
  54.5 3.6 %copy-start.7 = (f32[256]{0:T(256)S(1)}, f32[256]{0:T(256)}, u32[]{:S(2)}) copy-start(f32[256]{0:T(256)} %damping.1) | copy-start | bytes 3076
  54.5 7.7 %copy-start.5 = (f32[8,256]{1,0:T(8,128)S(1)}, f32[8,256]{1,0:T(8,128)}, u32[]{:S(2)}) copy-start(f32[8,256]{1,0:T(8,128)} %obsw.3) | copy-start | bytes 24580
  54.6 7.6 %collective-permute-start.2 = (f32[16,8,256]{2,1,0:T(8,128)S(1)}, f32[16,8,256]{2,1,0:T(8,128)S(1)}, u32[]{:S(2)}, u32[]{:S(2)}) collective-permute-start(f32[16,8,256]{2,1,0:T(8,128)S(1)} %get-tuple-element.20.keep), channel_id=1, source_target_pairs={{0,96},{96,0},{32,64},{64,32},{1,97},{97,1},{33,65},{65,33},{2,98}... | collective-permute-start | bytes 393224 | tf_op jit(solution)/shard_map/ppermute | solution.py:262
  58.3 13.9 %collective-permute-start.3 = (f32[16,8,256]{2,1,0:T(8,128)S(1)}, f32[16,8,256]{2,1,0:T(8,128)S(1)}, u32[]{:S(2)}, u32[]{:S(2)}) collective-permute-start(f32[16,8,256]{2,1,0:T(8,128)S(1)} %get-tuple-element.22.inner), channel_id=1, source_target_pairs={{0,96},{96,0},{32,64},{64,32},{1,97},{97,1},{33,65},{65,33},{2,98}... | collective-permute-start | bytes 393224 | tf_op jit(solution)/shard_map/ppermute | solution.py:263
  62.9 9.7 %collective-permute-start.4 = (f32[65,256]{1,0:T(8,128)S(1)}, f32[65,256]{1,0:T(8,128)S(1)}, u32[]{:S(2)}, u32[]{:S(2)}) collective-permute-start(f32[65,256]{1,0:T(8,128)S(1)} %get-tuple-element.23), channel_id=1, source_target_pairs={{0,31},{1,2},{2,1},{3,4},{4,3},{5,6},{6,5},{7,8},{8,7},{9,10},{10,... | collective-permute-start | bytes 199688 | tf_op jit(solution)/shard_map/ppermute | solution.py:227
  70.3 3.2 %collective-permute-start.5 = (f32[65,256]{1,0:T(8,128)S(1)}, f32[65,256]{1,0:T(8,128)S(1)}, u32[]{:S(2)}, u32[]{:S(2)}) collective-permute-start(f32[65,256]{1,0:T(8,128)S(1)} %get-tuple-element.24), channel_id=1, source_target_pairs={{0,1},{1,0},{2,3},{3,2},{4,5},{5,4},{6,7},{7,6},{8,9},{9,8},{10,11... | collective-permute-start | bytes 199688 | tf_op jit(solution)/shard_map/ppermute | solution.py:228
  75.4 30.3 %copy-start.2 = (bf16[2,256,8,256]{3,2,1,0:T(8,128)(2,1)S(1)}, bf16[2,256,8,256]{3,2,1,0:T(8,128)(2,1)}, u32[]{:S(2)}) copy-start(bf16[2,256,8,256]{3,2,1,0:T(8,128)(2,1)} %ens.3) | copy-start | bytes 6291460
  105.7 28.6 %copy-start.4 = (f32[2,8,256]{2,1,0:T(8,128)S(1)}, f32[2,8,256]{2,1,0:T(8,128)}, u32[]{:S(2)}) copy-start(f32[2,8,256]{2,1,0:T(8,128)} %control.3) | copy-start | bytes 49156
  107.3 27.0 %all-to-all-start.2 = ((f32[32,2,128]{2,1,0:T(2,128)}), f32[32,2,128]{2,1,0:T(2,128)S(1)}, u32[]{:S(2)}, u32[]{:S(2)}) async-start(f32[32,2,128]{2,1,0:T(2,128)} %get-tuple-element.27), calls=%async_computation.2 | async-start | bytes 65536 | tf_op jit(solution)/shard_map/all_to_all | solution.py:282
  119.8 11.7 %collective-permute-start.7 = (f32[2,8,256]{2,1,0:T(8,128)S(1)}, f32[2,8,256]{2,1,0:T(8,128)S(1)}, u32[]{:S(2)}, u32[]{:S(2)}) collective-permute-start(f32[2,8,256]{2,1,0:T(8,128)S(1)} %get-tuple-element.26.send), channel_id=1, source_target_pairs={{0,31},{1,2},{2,1},{3,4},{4,3},{5,6},{6,5},{7,8},{8,7},{9,10},{10,... | collective-permute-start | bytes 49160 | tf_op jit(solution)/shard_map/ppermute | solution.py:227
  127.2 5.1 %collective-permute-start.6 = (f32[2,8,256]{2,1,0:T(8,128)S(1)}, f32[2,8,256]{2,1,0:T(8,128)S(1)}, u32[]{:S(2)}, u32[]{:S(2)}) collective-permute-start(f32[2,8,256]{2,1,0:T(8,128)S(1)} %get-tuple-element.26.send), channel_id=1, source_target_pairs={{0,1},{1,0},{2,3},{3,2},{4,5},{5,4},{6,7},{7,6},{8,9},{9,8},{10,11... | collective-permute-start | bytes 49160 | tf_op jit(solution)/shard_map/ppermute | solution.py:228

commit v5 on v4

--- a/solution.py
+++ b/solution.py
@@ -47,10 +47,10 @@
     return north, south
 
 
-def rate_of(pos, scal, m):
+def rate_of(band, scal, m):
     rate = scal[2]
     for b in range(1, scal.shape[0] - 2):
-        rate = jnp.where(pos[3 + m] == b, scal[2 + b], rate)
+        rate = jnp.where(band[m] == b, scal[2 + b], rate)
     return rate
 
 
@@ -81,10 +81,10 @@
         copy.wait()
 
 
-def start_kernel(pos, scal, control, far, near, ens, loc_o, part_o):
+def start_kernel(pos, band, scal, control, far, near, ens, loc_o, part_o):
     scaled = []
     for m in range(2):
-        loc = sweeps(strips(pos[0] == 0, control[m], near[m], far[m]), rate_of(pos, scal, m))
+        loc = sweeps(strips(pos[0] == 0, control[m], near[m], far[m]), rate_of(band, scal, m))
         loc_o[m] = loc
         scaled.append(scal[m] * loc)
     n = part_o.shape[1]
@@ -211,10 +211,10 @@
         sums_o[:, m : m + 1] = jnp.broadcast_to(cells[None], (32, 1, 128))
 
 
-def end_kernel(scale, pos, scal, control, send, near, far, sums, out_o, weight_o):
+def end_kernel(scale, pos, band, scal, control, send, near, far, sums, out_o, weight_o):
     for m in range(2):
         out_o[m] = control[m] + sweeps(
-            strips(pos[0] == 0, send[m], near[m], far[m]), rate_of(pos, scal, m)
+            strips(pos[0] == 0, send[m], near[m], far[m]), rate_of(band, scal, m)
         )
     total = jnp.sum(sums[...], axis=0)
     for m in range(2):
@@ -235,7 +235,7 @@
     n = ensemble.shape[1] // 8
     ix, zp, zq, core = (lax.axis_index(a) for a in ("x", "zp", "zq", "core"))
     own = lax.bitwise_xor(zp, zq) * 4 + ix
-    pos = jnp.concatenate([jnp.stack([core, own, zp * 4]).astype(jnp.int32), member_band])
+    pos = jnp.stack([core, own, zp * 4]).astype(jnp.int32)
     scal = jnp.concatenate([weights, spread])
     strip2, planes, rows = (2, 8, 256), (n, 8, 256), (2 * n + 1, 256)
     halves, blocks = (n // 2, 8, 256), (8, n, 8, 256)
@@ -253,7 +253,7 @@
     )(ensemble, control)
     near0, far0 = swap_tiles(control, control)
     loc, parts = call(
-        start_kernel, "start", ([pos, scal], [own_control, far0, near0, ens]), [strip2, blocks]
+        start_kernel, "start", ([pos, member_band, scal], [own_control, far0, near0, ens]), [strip2, blocks]
     )
     parts, offset = lax.optimization_barrier((parts, (own * n).astype(jnp.uint32)))
     parts = lax.all_to_all(parts, GROUP, 0, 0, tiled=True)
@@ -285,12 +285,12 @@
         pl.pallas_call(
             functools.partial(end_kernel, 1.0 / math.sqrt(cells)),
             grid=(1,),
-            in_specs=[smem(), smem()] + [whole(strip2)] * 4 + [whole(sums.shape)],
+            in_specs=[smem(), smem(), smem()] + [whole(strip2)] * 4 + [whole(sums.shape)],
             out_specs=[whole(strip2), smem()],
             out_shape=[jax.ShapeDtypeStruct(strip2, F32), jax.ShapeDtypeStruct((2,), F32)],
             compiler_params=pltpu.CompilerParams(vmem_limit_bytes=40 * 2**20),
             name="end",
-        )(pos, scal, control, send, near, far, sums)
+        )(pos, member_band, scal, control, send, near, far, sums)
     )
 
 

time: 137 us -> 137 us (level)
  no operation moved by 1% of the time
where the time goes in v5:
time: 137 us; the launch traced here: 136 us
  blocking collectives  60.2 us (44%)
  starting transfers between devices  59.8 us (44%)
  Pallas kernels  7.97 us (6%)
  waiting for transfers between devices  4.23 us (3%)
  local copies, waits for them, and re-layouts  2.46 us (2%)
    all_to_all x1, blocking collectives, per_device(): grad = lax.all_to_all(grad, GROUP, 0, 0, tiled=True)  30.2 us
    all_to_all x1, blocking collectives, per_device(): parts = lax.all_to_all(parts, GROUP, 0, 0, tiled=True)  30.1 us
    ppermute x3, starting transfers between devices, swap_tiles(): far = lax.ppermute(far, TILE, far_pairs)  25.1 us
    ppermute x3, starting transfers between devices, swap_tiles(): near = lax.ppermute(near, TILE, [(i, i ^ 1) for i in range(n)])  14 us
    all_to_all x1, starting transfers between devices, per_device(): sums = lax.all_to_all(sums, TILE, 0, 0, tiled=True)  13.5 us
    pallas_call x5, Pallas kernels, call(): pl.pallas_call(body, in_specs=[smem() for _ in scalars] + [vmem for _ in...  6 us
    ppermute x1, starting transfers between devices, per_device(): got_inner = lax.ppermute(inner, ('zp', 'zq'), across)  3.57 us
    ppermute x1, starting transfers between devices, per_device(): got_edge = lax.ppermute(edge, ('zp', 'zq'), across)  3.5 us
  transfers between devices with their start and end apart: 9, of which 5 were waited for; matrix products, arithmetic and copies ran while one was open for 1% of the time, Pallas kernels for 1%

profile of v5, /device:TPU:1, one launch (start us, length us, event | category | flops | bytes accessed | tf_op | source)
XLA Modules:
  0.0 136.4 jit_solution(8076030593621528213)
XLA Ops:
  0.6 0.0 copy-start
  0.7 10.3 %collective-permute-start = (f32[2,8,256]{2,1,0:T(8,128)}, f32[2,8,256]{2,1,0:T(8,128)S(1)}, u32[]{:S(2)}, u32[]{:S(2)}) collective-permute-start(f32[2,8,256]{2,1,0:T(8,128)} %control.3), channel_id=1, source_target_pairs={{0,31},{1,2},{2,1},{3,4},{4,3},{5,6},{6,5},{7,8},{8,7},{9,10},{10,... | collective-permute-start | bytes 49160 | tf_op jit(solution)/shard_map/ppermute | solution.py:227
  11.0 7.8 %collective-permute-start.1 = (f32[2,8,256]{2,1,0:T(8,128)}, f32[2,8,256]{2,1,0:T(8,128)S(1)}, u32[]{:S(2)}, u32[]{:S(2)}) collective-permute-start(f32[2,8,256]{2,1,0:T(8,128)} %control.3), channel_id=1, source_target_pairs={{0,1},{1,0},{2,3},{3,2},{4,5},{5,4},{6,7},{7,6},{8,9},{9,8},{10,11... | collective-permute-start | bytes 49160 | tf_op jit(solution)/shard_map/ppermute | solution.py:228
  18.9 0.7 pad_maximum_fusion.scal
  19.6 0.1 pad_add_fusion.pos
  19.7 1.6 %copy-done.1 = bf16[2,256,8,256]{3,2,1,0:T(8,128)(2,1)S(1)} copy-done((bf16[2,256,8,256]{3,2,1,0:T(8,128)(2,1)S(1)}, bf16[2,256,8,256]{3,2,1,0:T(8,128)(2,1)}, u32[]{:S(2)}) %copy-start.1) | copy-done | bytes 2097176
  21.3 0.7 copy-done.3
  22.0 0.2 bring.1
  22.2 0.0 collective-permute-done.far
  22.2 1.6 %start.1 = (f32[2,8,256]{2,1,0:T(8,128)S(1)}, f32[8,32,8,256]{3,2,1,0:T(8,128)S(1)}) custom-call(s32[3]{0:T(128)S(1)} %pad_add_fusion.pos, s32[2]{0:T(128)S(1)} %copy-done.8, f32[6]{0:T(128)S(1)} %pad_maximum_fusion.scal, f32[2,8,256]{2,1,0:T(8,128)S(1)} %get-tuple-element.15.control, f32[2,8,256]{2,1,0:T(8,128)S(1)} %collective-permute-done.far, ...), custom_call_target="tpu_custom_call" | custom-call | tf_op jit(solution)/shard_map/start/pallas_call | solution.py:31
  23.8 30.1 %all_to_all.15.parts = f32[8,32,8,256]{3,2,1,0:T(8,128)S(1)} all-to-all(f32[8,32,8,256]{3,2,1,0:T(8,128)S(1)} %get-tuple-element.19), channel_id=1, replica_groups=mesh['x'=4,'zp'=2,'zq'=2,'y'=4,'zh'=4,'core'=2] {'zq','x'}, dimensions={0} | all-to-all | bytes 4194304 | tf_op jit(solution)/shard_map/all_to_all | solution.py:259
  53.9 0.1 mid.1
  54.0 3.5 %collective-permute-start.2 = (f32[16,8,256]{2,1,0:T(8,128)S(1)}, f32[16,8,256]{2,1,0:T(8,128)S(1)}, u32[]{:S(2)}, u32[]{:S(2)}) collective-permute-start(f32[16,8,256]{2,1,0:T(8,128)S(1)} %get-tuple-element.20.keep), channel_id=1, source_target_pairs={{0,96},{96,0},{32,64},{64,32},{1,97},{97,1},{33,65},{65,33},{2,98}... | collective-permute-start | bytes 393224 | tf_op jit(solution)/shard_map/ppermute | solution.py:262
  57.5 0.1 fusion
  57.6 0.1 copy.15
  57.7 3.6 %collective-permute-start.3 = (f32[16,8,256]{2,1,0:T(8,128)S(1)}, f32[16,8,256]{2,1,0:T(8,128)S(1)}, u32[]{:S(2)}, u32[]{:S(2)}) collective-permute-start(f32[16,8,256]{2,1,0:T(8,128)S(1)} %get-tuple-element.22.inner), channel_id=1, source_target_pairs={{0,96},{96,0},{32,64},{64,32},{1,97},{97,1},{33,65},{65,33},{2,98}... | collective-permute-start | bytes 393224 | tf_op jit(solution)/shard_map/ppermute | solution.py:263
  61.3 0.3 collective-permute-done.2.got
  61.6 0.7 edge.1
  62.3 7.4 %collective-permute-start.4 = (f32[65,256]{1,0:T(8,128)S(1)}, f32[65,256]{1,0:T(8,128)S(1)}, u32[]{:S(2)}, u32[]{:S(2)}) collective-permute-start(f32[65,256]{1,0:T(8,128)S(1)} %get-tuple-element.23), channel_id=1, source_target_pairs={{0,31},{1,2},{2,1},{3,4},{4,3},{5,6},{6,5},{7,8},{8,7},{9,10},{10,... | collective-permute-start | bytes 199688 | tf_op jit(solution)/shard_map/ppermute | solution.py:227
  69.7 1.9 %collective-permute-start.5 = (f32[65,256]{1,0:T(8,128)S(1)}, f32[65,256]{1,0:T(8,128)S(1)}, u32[]{:S(2)}, u32[]{:S(2)}) collective-permute-start(f32[65,256]{1,0:T(8,128)S(1)} %get-tuple-element.24), channel_id=1, source_target_pairs={{0,1},{1,0},{2,3},{3,2},{4,5},{5,4},{6,7},{7,6},{8,9},{9,8},{10,11... | collective-permute-start | bytes 199688 | tf_op jit(solution)/shard_map/ppermute | solution.py:228
  71.6 0.3 collective-permute-done.4.far
  71.9 0.9 collective-permute-done.5.near
  72.8 1.9 %dynamics.1 = f32[8,32,8,256]{3,2,1,0:T(8,128)S(1)} custom-call(s32[3]{0:T(128)S(1)} %pad_add_fusion.pos, f32[2,256]{1,0:T(2,128)S(1)} %copy-done.6, f32[256]{0:T(256)S(1)} %copy-done.7, f32[16,8,256]{2,1,0:T(8,128)S(1)} %get-tuple-element.21.edge, f32[16,8,256]{2,1,0:T(8,128)S(1)} %get-tuple-element.22.inner, f32[16,8,256]{2,1,0:T(8,128)S(1)} %collective-permute-done.3.got, ...), custom_call_target="tpu_custom_call" | custom-call | tf_op jit(solution)/shard_map/dynamics/pallas_call | solution.py:31
  74.8 0.0 copy-start.2
  74.8 30.2 %all_to_all.16.grad = f32[8,32,8,256]{3,2,1,0:T(8,128)S(1)} all-to-all(f32[8,32,8,256]{3,2,1,0:T(8,128)S(1)} %dynamics.1), channel_id=1, replica_groups=mesh['x'=4,'zp'=2,'zq'=2,'y'=4,'zh'=4,'core'=2] {'zq','x'}, dimensions={0} | all-to-all | bytes 4194304 | tf_op jit(solution)/shard_map/all_to_all | solution.py:277
  105.0 1.6 %project.1 = (f32[2,8,256]{2,1,0:T(8,128)S(1)}, f32[32,2,128]{2,1,0:T(2,128)}) custom-call(s32[3]{0:T(128)S(1)} %pad_add_fusion.pos, f32[6]{0:T(128)S(1)} %pad_maximum_fusion.scal, f32[8,32,8,256]{3,2,1,0:T(8,128)S(1)} %all_to_all.16.grad, bf16[2,256,8,256]{3,2,1,0:T(8,128)(2,1)S(1)} %copy-done.2, f32[2,8,256]{2,1,0:T(8,128)S(1)} %get-tuple-element.25.loc), custom_call_target="tpu_custom_call" | custom-call | tf_op jit(solution)/shard_map/project/pallas_call | solution.py:31
  106.6 13.5 %all-to-all-start.2 = ((f32[32,2,128]{2,1,0:T(2,128)}), f32[32,2,128]{2,1,0:T(2,128)S(1)}, u32[]{:S(2)}, u32[]{:S(2)}) async-start(f32[32,2,128]{2,1,0:T(2,128)} %get-tuple-element.27), calls=%async_computation.2 | async-start | bytes 65536 | tf_op jit(solution)/shard_map/all_to_all | solution.py:282
  120.2 7.4 %collective-permute-start.7 = (f32[2,8,256]{2,1,0:T(8,128)S(1)}, f32[2,8,256]{2,1,0:T(8,128)S(1)}, u32[]{:S(2)}, u32[]{:S(2)}) collective-permute-start(f32[2,8,256]{2,1,0:T(8,128)S(1)} %get-tuple-element.26.send), channel_id=1, source_target_pairs={{0,31},{1,2},{2,1},{3,4},{4,3},{5,6},{6,5},{7,8},{8,7},{9,10},{10,... | collective-permute-start | bytes 49160 | tf_op jit(solution)/shard_map/ppermute | solution.py:227
  127.6 4.3 %collective-permute-start.6 = (f32[2,8,256]{2,1,0:T(8,128)S(1)}, f32[2,8,256]{2,1,0:T(8,128)S(1)}, u32[]{:S(2)}, u32[]{:S(2)}) collective-permute-start(f32[2,8,256]{2,1,0:T(8,128)S(1)} %get-tuple-element.26.send), channel_id=1, source_target_pairs={{0,1},{1,0},{2,3},{3,2},{4,5},{5,4},{6,7},{7,6},{8,9},{9,8},{10,11... | collective-permute-start | bytes 49160 | tf_op jit(solution)/shard_map/ppermute | solution.py:228
  131.9 0.8 collective-permute-done.6.near
  132.7 1.9 %all-to-all-done.2.sums = f32[32,2,128]{2,1,0:T(2,128)S(1)} async-done(((f32[32,2,128]{2,1,0:T(2,128)}), f32[32,2,128]{2,1,0:T(2,128)S(1)}, u32[]{:S(2)}, u32[]{:S(2)}) %all-to-all-start.2) | async-done | bytes 32800 | tf_op jit(solution)/shard_map/all_to_all | solution.py:282
  134.6 1.8 %end.1 = (f32[2,8,256]{2,1,0:T(8,128)}, f32[2]{0:T(128)}) custom-call(s32[3]{0:T(128)S(1)} %pad_add_fusion.pos, s32[2]{0:T(128)S(1)} %copy-done.8, f32[6]{0:T(128)S(1)} %pad_maximum_fusion.scal, f32[2,8,256]{2,1,0:T(8,128)S(1)} %copy-done.4, f32[2,8,256]{2,1,0:T(8,128)S(1)} %get-tuple-element.26.send, f32[2,8,256]{2,1,0:T(8,128)S(1)} %collective-permute-done.6.near, ...), custom_call_target="tpu_custom_call" | custom-call | tf_op jit(solution)/shard_map/end/pallas_call | solution.py:285
  (18 shorter events, 0.1 us)
Async XLA Ops:
  0.6 60.7 %copy-start = (f32[256,8,256]{2,1,0:T(8,128)S(1)}, f32[256,8,256]{2,1,0:T(8,128)}, u32[]{:S(2)}) copy-start(f32[256,8,256]{2,1,0:T(8,128)} %param.16) | copy-start | bytes 6291460
  0.6 21.6 %copy-start.8 = (s32[2]{0:T(128)S(1)}, s32[2]{0:T(128)}, u32[]{:S(2)}) copy-start(s32[2]{0:T(128)} %band.3) | copy-start | bytes 28
  0.7 21.5 %collective-permute-start = (f32[2,8,256]{2,1,0:T(8,128)}, f32[2,8,256]{2,1,0:T(8,128)S(1)}, u32[]{:S(2)}, u32[]{:S(2)}) collective-permute-start(f32[2,8,256]{2,1,0:T(8,128)} %control.3), channel_id=1, source_target_pairs={{0,31},{1,2},{2,1},{3,4},{4,3},{5,6},{6,5},{7,8},{8,7},{9,10},{10,... | collective-permute-start | bytes 49160 | tf_op jit(solution)/shard_map/ppermute | solution.py:227
  11.0 11.2 %collective-permute-start.1 = (f32[2,8,256]{2,1,0:T(8,128)}, f32[2,8,256]{2,1,0:T(8,128)S(1)}, u32[]{:S(2)}, u32[]{:S(2)}) collective-permute-start(f32[2,8,256]{2,1,0:T(8,128)} %control.3), channel_id=1, source_target_pairs={{0,1},{1,0},{2,3},{3,2},{4,5},{5,4},{6,7},{7,6},{8,9},{9,8},{10,11... | collective-permute-start | bytes 49160 | tf_op jit(solution)/shard_map/ppermute | solution.py:228
  19.7 1.6 %copy-start.1 = (bf16[2,256,8,256]{3,2,1,0:T(8,128)(2,1)S(1)}, bf16[2,256,8,256]{3,2,1,0:T(8,128)(2,1)}, u32[]{:S(2)}) copy-start(bf16[2,256,8,256]{3,2,1,0:T(8,128)(2,1)} %ens.3) | copy-start | bytes 6291460
  21.3 0.7 copy-start.3
  53.9 3.6 %copy-start.6 = (f32[2,256]{1,0:T(2,128)S(1)}, f32[2,256]{1,0:T(2,128)}, u32[]{:S(2)}) copy-start(f32[2,256]{1,0:T(2,128)} %advect.1) | copy-start | bytes 6148
  53.9 3.6 %copy-start.7 = (f32[256]{0:T(256)S(1)}, f32[256]{0:T(256)}, u32[]{:S(2)}) copy-start(f32[256]{0:T(256)} %damping.1) | copy-start | bytes 3076
  53.9 7.7 %copy-start.5 = (f32[8,256]{1,0:T(8,128)S(1)}, f32[8,256]{1,0:T(8,128)}, u32[]{:S(2)}) copy-start(f32[8,256]{1,0:T(8,128)} %obsw.3) | copy-start | bytes 24580
  54.0 7.6 %collective-permute-start.2 = (f32[16,8,256]{2,1,0:T(8,128)S(1)}, f32[16,8,256]{2,1,0:T(8,128)S(1)}, u32[]{:S(2)}, u32[]{:S(2)}) collective-permute-start(f32[16,8,256]{2,1,0:T(8,128)S(1)} %get-tuple-element.20.keep), channel_id=1, source_target_pairs={{0,96},{96,0},{32,64},{64,32},{1,97},{97,1},{33,65},{65,33},{2,98}... | collective-permute-start | bytes 393224 | tf_op jit(solution)/shard_map/ppermute | solution.py:262
  57.7 13.9 %collective-permute-start.3 = (f32[16,8,256]{2,1,0:T(8,128)S(1)}, f32[16,8,256]{2,1,0:T(8,128)S(1)}, u32[]{:S(2)}, u32[]{:S(2)}) collective-permute-start(f32[16,8,256]{2,1,0:T(8,128)S(1)} %get-tuple-element.22.inner), channel_id=1, source_target_pairs={{0,96},{96,0},{32,64},{64,32},{1,97},{97,1},{33,65},{65,33},{2,98}... | collective-permute-start | bytes 393224 | tf_op jit(solution)/shard_map/ppermute | solution.py:263
  62.3 9.6 %collective-permute-start.4 = (f32[65,256]{1,0:T(8,128)S(1)}, f32[65,256]{1,0:T(8,128)S(1)}, u32[]{:S(2)}, u32[]{:S(2)}) collective-permute-start(f32[65,256]{1,0:T(8,128)S(1)} %get-tuple-element.23), channel_id=1, source_target_pairs={{0,31},{1,2},{2,1},{3,4},{4,3},{5,6},{6,5},{7,8},{8,7},{9,10},{10,... | collective-permute-start | bytes 199688 | tf_op jit(solution)/shard_map/ppermute | solution.py:227
  69.7 3.2 %collective-permute-start.5 = (f32[65,256]{1,0:T(8,128)S(1)}, f32[65,256]{1,0:T(8,128)S(1)}, u32[]{:S(2)}, u32[]{:S(2)}) collective-permute-start(f32[65,256]{1,0:T(8,128)S(1)} %get-tuple-element.24), channel_id=1, source_target_pairs={{0,1},{1,0},{2,3},{3,2},{4,5},{5,4},{6,7},{7,6},{8,9},{9,8},{10,11... | collective-permute-start | bytes 199688 | tf_op jit(solution)/shard_map/ppermute | solution.py:228
  74.8 30.2 %copy-start.2 = (bf16[2,256,8,256]{3,2,1,0:T(8,128)(2,1)S(1)}, bf16[2,256,8,256]{3,2,1,0:T(8,128)(2,1)}, u32[]{:S(2)}) copy-start(bf16[2,256,8,256]{3,2,1,0:T(8,128)(2,1)} %ens.3) | copy-start | bytes 6291460
  105.0 29.7 %copy-start.4 = (f32[2,8,256]{2,1,0:T(8,128)S(1)}, f32[2,8,256]{2,1,0:T(8,128)}, u32[]{:S(2)}) copy-start(f32[2,8,256]{2,1,0:T(8,128)} %control.3) | copy-start | bytes 49156
  106.6 28.0 %all-to-all-start.2 = ((f32[32,2,128]{2,1,0:T(2,128)}), f32[32,2,128]{2,1,0:T(2,128)S(1)}, u32[]{:S(2)}, u32[]{:S(2)}) async-start(f32[32,2,128]{2,1,0:T(2,128)} %get-tuple-element.27), calls=%async_computation.2 | async-start | bytes 65536 | tf_op jit(solution)/shard_map/all_to_all | solution.py:282
  120.2 11.7 %collective-permute-start.7 = (f32[2,8,256]{2,1,0:T(8,128)S(1)}, f32[2,8,256]{2,1,0:T(8,128)S(1)}, u32[]{:S(2)}, u32[]{:S(2)}) collective-permute-start(f32[2,8,256]{2,1,0:T(8,128)S(1)} %get-tuple-element.26.send), channel_id=1, source_target_pairs={{0,31},{1,2},{2,1},{3,4},{4,3},{5,6},{6,5},{7,8},{8,7},{9,10},{10,... | collective-permute-start | bytes 49160 | tf_op jit(solution)/shard_map/ppermute | solution.py:227
  127.6 5.1 %collective-permute-start.6 = (f32[2,8,256]{2,1,0:T(8,128)S(1)}, f32[2,8,256]{2,1,0:T(8,128)S(1)}, u32[]{:S(2)}, u32[]{:S(2)}) collective-permute-start(f32[2,8,256]{2,1,0:T(8,128)S(1)} %get-tuple-element.26.send), channel_id=1, source_target_pairs={{0,1},{1,0},{2,3},{3,2},{4,5},{5,4},{6,7},{7,6},{8,9},{9,8},{10,11... | collective-permute-start | bytes 49160 | tf_op jit(solution)/shard_map/ppermute | solution.py:228
